TPU v7x, 32 devices: a whole 2x2x4 slice. The times are simulated.
32 devices in a mesh: member: 8 (over y, x, core), dp: 4 (over z).
Axes of the slice: x: 2, y: 2, z: 4, core: 2. Of those that a mesh axis runs over, the one named last changes fastest.
Arguments:
- teacher_tokens: bfloat16 [2752, 1536], P('dp'), may hold values from -100 to 100
- teacher_qkv: bfloat16 [8, 1536, 4608], P('member', None, 'dp'), may hold values from -0.15625 to 0.15625
- student_tokens: bfloat16 [2752, 1024], P('dp'), may hold values from -6 to 6
- student_gain: float32 [1024], replicated, may hold values from 0.1 to 1.9
- w_up: bfloat16 [1024, 4096], P(None, 'member'), may hold values from -0.1875 to 0.1875
- w_down: bfloat16 [1024, 4096], P(None, 'member'), may hold values from -0.09375 to 0.09375
- w_head: bfloat16 [1024, 1536], P(None, 'member'), may hold values from -0.1875 to 0.1875
Outputs:
- grad_up: float32 [1024, 4096], P('dp', 'member')
- grad_down: float32 [1024, 4096], P('dp', 'member')
- grad_head: float32 [1024, 1536], P('dp', 'member')
All inputs are finite; a program needn't handle non-finite values.
Results may differ from a plain program's by a relative error of at most 0.0055.
Values may be sent and summed in bfloat16 or wider, within the bound.
A program may use at most 320 MiB of HBM per device.

v0:
```python
from functools import partial
import math

import jax
import jax.numpy as jnp
from jax import lax
from jax.sharding import PartitionSpec as P

VALID = 1370
IMAGES = 2


def body(teacher_tokens, teacher_qkv, student_tokens, student_gain, w_up, w_down, w_head):
    tok_rows = teacher_tokens.shape[0]
    feat_width = teacher_tokens.shape[1]
    head_count = feat_width // 64
    own_columns = teacher_qkv[0]
    query_slots = lax.axis_index("dp") * tok_rows + jnp.arange(tok_rows, dtype=jnp.int32)
    query_image = query_slots % IMAGES
    real_query = query_slots // IMAGES < VALID
    projected = jnp.dot(
        teacher_tokens,
        lax.all_gather(own_columns, "dp", axis=1, tiled=True),
        preferred_element_type=jnp.float32,
    ).astype(jnp.bfloat16)
    queries = projected[:, :feat_width].reshape(tok_rows, head_count, 64)
    keys_local = projected[:, feat_width : 2 * feat_width]
    values_local = projected[:, 2 * feat_width :]
    row_max = jnp.full((head_count, tok_rows), -1e30, jnp.float32)
    weighted = jnp.zeros((tok_rows, head_count, 64), jnp.float32)
    key_heads = lax.all_gather(keys_local, "dp", axis=0, tiled=True).reshape(-1, head_count, 64)
    value_heads = lax.all_gather(values_local, "dp", axis=0, tiled=True).reshape(-1, head_count, 64)
    key_slots = jnp.arange(key_heads.shape[0], dtype=jnp.int32)
    allowed = (query_image[:, None] == (key_slots % IMAGES)[None, :]) & (
        key_slots // IMAGES < VALID
    )[None, :]
    scores = (
        jnp.einsum("qhd,khd->hqk", queries, key_heads, preferred_element_type=jnp.float32) * 0.125
    )
    scores = jnp.where(allowed[None], scores, -1e30)
    new_max = jnp.maximum(row_max, jnp.max(scores, axis=-1))
    factor = jnp.exp(row_max - new_max)
    expsc = jnp.where(allowed[None], jnp.exp(scores - new_max[:, :, None]), 0.0)
    denom_sum = jnp.sum(expsc, axis=-1)
    update = jnp.einsum(
        "hqk,khd->qhd", expsc.astype(jnp.bfloat16), value_heads, preferred_element_type=jnp.float32
    )
    weighted = weighted * factor.T[:, :, None] + update
    row_max, denom_sum, weighted = (new_max, denom_sum, weighted)
    context = (weighted / denom_sum.T[:, :, None]).reshape(tok_rows, feat_width)
    member_slot = lax.axis_index("member")
    share_width = feat_width // lax.axis_size("member")
    summed = lax.psum(context, "member")
    row_mean = jnp.mean(summed, axis=-1, keepdims=True)
    mean_square = jnp.mean(summed * summed, axis=-1, keepdims=True)
    full_target = (summed - row_mean) * lax.rsqrt(mean_square - row_mean * row_mean + 1e-06)
    target = lax.dynamic_slice_in_dim(full_target, member_slot * share_width, share_width, 1)
    inputs = student_tokens.astype(jnp.float32)
    in_mean = jnp.mean(inputs, axis=-1, keepdims=True)
    in_var = jnp.mean((inputs - in_mean) ** 2, axis=-1, keepdims=True)
    normed = ((inputs - in_mean) * lax.rsqrt(in_var + 1e-06) * student_gain).astype(jnp.bfloat16)
    pre = jnp.dot(normed, w_up, preferred_element_type=jnp.float32)
    gelu_tanh = partial(jax.nn.gelu, approximate=True)
    hidden = gelu_tanh(pre).astype(jnp.bfloat16)
    branch_part = lax.dot_general(
        hidden, w_down, (((1,), (1,)), ((), ())), preferred_element_type=jnp.float32
    )
    student_out = (inputs + lax.psum(branch_part, "member")).astype(jnp.bfloat16)
    pred = jnp.dot(student_out, w_head, preferred_element_type=jnp.float32)
    pred_grad = jnp.where(
        real_query[:, None], (pred - target) / math.sqrt(IMAGES * VALID), 0.0
    ).astype(jnp.bfloat16)
    grad_head = lax.dot_general(
        student_out, pred_grad, (((0,), (0,)), ((), ())), preferred_element_type=jnp.float32
    )
    out_part = lax.dot_general(
        pred_grad, w_head, (((1,), (1,)), ((), ())), preferred_element_type=jnp.float32
    )
    out_grad = lax.psum(out_part, "member").astype(jnp.bfloat16)
    grad_down = lax.dot_general(
        out_grad, hidden, (((0,), (0,)), ((), ())), preferred_element_type=jnp.float32
    )
    hidden_grad = jnp.dot(out_grad, w_down, preferred_element_type=jnp.float32)
    _, pullback = jax.vjp(gelu_tanh, pre)
    pre_grad = pullback(hidden_grad)[0].astype(jnp.bfloat16)
    grad_up = lax.dot_general(
        normed, pre_grad, (((0,), (0,)), ((), ())), preferred_element_type=jnp.float32
    )
    grad_up, grad_down, grad_head = (
        lax.psum_scatter(grad_up, "dp", scatter_dimension=0, tiled=True),
        lax.psum_scatter(grad_down, "dp", scatter_dimension=0, tiled=True),
        lax.psum_scatter(grad_head, "dp", scatter_dimension=0, tiled=True),
    )
    return (grad_up, grad_down, grad_head)


def solution(mesh):
    in_specs = (
        P("dp", None),
        P("member", None, "dp"),
        P("dp", None),
        P(),
        P(None, "member"),
        P(None, "member"),
        P(None, "member"),
    )
    out_specs = (P("dp", "member"), P("dp", "member"), P("dp", "member"))
    return jax.shard_map(body, mesh=mesh, in_specs=in_specs, out_specs=out_specs, check_vma=False)
```

profile of v0, /device:TPU:0, one launch (start us, length us, event | category | flops | bytes accessed | tf_op | source)
XLA Modules:
  0.0 943.8 jit_solution(12835223692961296576)
XLA Ops:
  7.2 0.7 all-gather.9.cloned.1.call-update
  8.0 248.3 %all-gather.9.cloned.1.call-done = bf16[1,1536,4608]{2,1,0:T(8,128)(2,1)} async-done(((bf16[1,1536,1152]{2,1,0:T(8,128)(2,1)}), bf16[1,1536,4608]{2,1,0:T(8,128)(2,1)}) %all-gather.9.cloned.1.call-update) | async-done | bytes 14155792 | tf_op jit(solution)/shard_map/all_gather | solution.py:23
  256.2 13.2 %fusion.8 = bf16[688,4608]{1,0:T(8,128)(2,1)S(1)} fusion(bf16[688,1536]{1,0:T(8,128)(2,1)S(1)} %copy-done, bf16[1,1536,4608]{2,1,0:T(8,128)(2,1)} %all-gather.9.cloned.1.call-done), kind=kOutput, calls=%fused_computation.9 | convolution fusion | flops 9742344192 | bytes 22609920 | tf_op jit(solution)/shard_map/dot_general | solution.py:21
  269.4 2.8 fusion.73
  272.3 0.0 all-gather.7.cloned.1.call-start
  272.4 1.2 copy-done.2
  273.6 0.3 convert_reduce_fusion
  273.9 0.5 fusion.14
  274.4 1.0 fusion.70
  275.4 1.1 copy-done.15
  276.5 2.6 fusion.68
  279.1 1.4 compare_and_fusion
  280.5 4.3 copy.13
  284.8 0.2 all-reduce.4.cloned.1.call-start
  285.0 136.3 %all-gather.5.cloned.1.call-done = bf16[2752,1536]{1,0:T(8,128)(2,1)} async-done(((bf16[688,1536]{1,0:T(8,128)(2,1)}), bf16[2752,1536]{1,0:T(8,128)(2,1)}) %all-gather.5.cloned.1.call-update) | async-done | bytes 8454160 | tf_op jit(solution)/shard_map/all_gather | solution.py:31
  421.3 12.1 %copy.14 = bf16[2752,1536]{0,1:T(8,128)(2,1)} copy(bf16[2752,1536]{1,0:T(8,128)(2,1)} %all-gather.5.cloned.1.call-done) | data formatting | bytes 16908288 | tf_op jit(solution)/shard_map/all_gather | solution.py:31
  433.5 66.7 %fusion = (f32[24,688]{1,0:T(8,128)S(1)}, f32[24,688,2752]{2,1,0:T(8,128)}) fusion(pred[688,2752]{1,0:T(8,128)(4,1)S(1)} %compare_and_fusion, bf16[688,24,64]{0,2,1:T(8,128)(2,1)} %bitcast.30, bf16[2752,24,64]{0,2,1:T(8,128)(2,1)} %bitcast.29), kind=kOutput, calls=%fused_computation.2 | convolution fusion | flops 5952757760 | bytes 194291200 | tf_op jit(solution)/shard_map/qhd,khd->hqk/dot_general | solution.py:38
  500.2 76.1 %fusion.1 = f32[24,688]{1,0:T(8,128)S(1)} fusion(f32[24,688,2752]{2,1,0:T(8,128)} %get-tuple-element.15, f32[24,688]{1,0:T(8,128)S(1)} %get-tuple-element.11, pred[688,2752]{1,0:T(8,128)(4,1)S(1)} %compare_and_fusion), kind=kLoop, calls=%fused_computation.3 | loop fusion | flops 227188608 | bytes 183789568 | tf_op jit(solution)/shard_map/reduce_sum | solution.py:44
  576.3 11.7 %copy.15 = bf16[2752,1536]{0,1:T(8,128)(2,1)} copy(bf16[2752,1536]{1,0:T(8,128)(2,1)} %all-gather.7.cloned.1.call-done) | data formatting | bytes 16908288 | tf_op jit(solution)/shard_map/all_gather | solution.py:32
  587.9 67.0 %fusion.11 = f32[688,24,64]{0,2,1:T(8,128)} fusion(f32[688,24]{0,1:T(8,128)S(1)} %bitcast.33, f32[688,24]{0,1:T(8,128)S(1)} %get-tuple-element.10, bf16[2752,24,64]{0,2,1:T(8,128)(2,1)} %bitcast.31, f32[24,688,2752]{2,1,0:T(8,128)} %get-tuple-element.15, f32[24,688]{1,0:T(8,128)S(1)} %get-tuple-element.11, pred[688,2752]{1,0:T(8,128)(4,1)S(1)} %compare_and_fusion), kind=kOutput, calls=%fused_computation.12 | convolution fusion | flops 6045769728 | bytes 196536832 | tf_op jit(solution)/shard_map/hqk,khd->qhd/dot_general | solution.py:45
  655.0 0.3 reduce-scatter.8.cloned.1.call-start
  655.3 116.1 %all-reduce.4.cloned.1.call-done = (f32[688,1536]{0,1:T(8,128)}, f32[688,1024]{1,0:T(8,128)}) async-done(((f32[688,1536]{0,1:T(8,128)}, f32[688,1024]{1,0:T(8,128)}), (f32[688,1536]{0,1:T(8,128)}, f32[688,1024]{1,0:T(8,128)})) %all-reduce.4.cloned.1.call-update) | async-done | bytes 7045136 | tf_op jit(solution)/shard_map/psum | solution.py:53
  771.4 3.1 fusion.72
  774.5 0.6 copy-done.4
  775.1 1.7 fusion.29
  776.8 1.4 fusion.65
  778.3 2.1 fusion.74
  780.5 62.0 %all-reduce.5 = bf16[688,1024]{1,0:T(8,128)(2,1)S(1)} all-reduce(f32[688,1024]{1,0:T(8,128)} %fusion.74), channel_id=1, replica_groups=mesh['member'=8,'dp'=4] {'member'}, use_global_device_ids=true, to_apply=%region_8.9 | all-reduce | flops 704512 | bytes 4227072 | tf_op jit(solution)/shard_map/psum | solution.py:79
  842.5 4.3 fusion.30
  846.9 5.9 fusion.37
  852.9 37.8 %reduce-scatter.6.cloned.1.call-done = f32[256,512]{1,0:T(8,128)} async-done(((f32[1024,512]{1,0:T(8,128)}), f32[256,512]{1,0:T(8,128)}) %reduce-scatter.6.cloned.1.call-update) | async-done | bytes 524304 | tf_op jit(solution)/shard_map/reduce_scatter | solution.py:91
  890.7 46.2 %reduce-scatter.4.cloned.1.call-done = f32[256,512]{1,0:T(8,128)} async-done(((f32[1024,512]{1,0:T(8,128)}), f32[256,512]{1,0:T(8,128)}) %reduce-scatter.4.cloned.1.call-update) | async-done | bytes 524304 | tf_op jit(solution)/shard_map/reduce_scatter | solution.py:90
  (49 shorter events, 0.5 us)
Async XLA Ops:
  7.2 249.1 %copy-start = (bf16[688,1536]{1,0:T(8,128)(2,1)S(1)}, bf16[688,1536]{1,0:T(8,128)(2,1)}, u32[]{:S(2)}) copy-start(bf16[688,1536]{1,0:T(8,128)(2,1)} %param.7) | copy-start | bytes 6340612
  7.2 249.1 %all-gather.9.cloned.1.call-start = ((), (), s32[]{:S(2)}) async-start(), calls=%async_computation.8 | async-start | bytes 17694720 | tf_op jit(solution)/shard_map/all_gather | solution.py:23
  7.9 413.4 %all-gather.5.cloned.1.call-start = ((), (), s32[]{:S(2)}) async-start(), calls=%async_computation.3 | async-start | bytes 10567680 | tf_op jit(solution)/shard_map/all_gather | solution.py:31
  272.3 1.4 copy-start.2
  272.3 2.1 copy-start.11
  272.3 2.1 copy-start.13
  272.3 304.0 %all-gather.7.cloned.1.call-start = ((), (), s32[]{:S(2)}) async-start(), calls=%async_computation.4 | async-start | bytes 10567680 | tf_op jit(solution)/shard_map/all_gather | solution.py:32
  273.9 1.5 copy-start.7
  274.4 1.0 copy-start.9
  274.4 2.1 copy-start.12
  275.4 1.1 copy-start.15
  284.8 486.6 %all-reduce.4.cloned.1.call-start = ((), (), s32[]{:S(2)}) async-start(), calls=%async_computation.9 | async-start | bytes 15073280 | tf_op jit(solution)/shard_map/psum | solution.py:53
  655.0 197.9 %reduce-scatter.8.cloned.1.call-start = ((), (), s32[]{:S(2)}) async-start(), calls=%async_computation.7 | async-start | bytes 983040 | tf_op jit(solution)/shard_map/reduce_scatter | solution.py:92
  771.4 3.1 copy-start.3
  771.4 3.6 copy-start.4
  771.4 3.7 copy-start.5
  780.4 110.3 %reduce-scatter.6.cloned.1.call-start = ((), (), s32[]{:S(2)}) async-start(), calls=%async_computation.6 | async-start | bytes 2621440 | tf_op jit(solution)/shard_map/reduce_scatter | solution.py:91
  842.4 4.4 copy-start.6
  842.4 4.5 copy-start.8
  842.5 4.5 copy-start.10
  842.5 4.5 copy-start.14
  846.8 90.1 %reduce-scatter.4.cloned.1.call-start = ((), (), s32[]{:S(2)}) async-start(), calls=%async_computation.5 | async-start | bytes 2621440 | tf_op jit(solution)/shard_map/reduce_scatter | solution.py:90
  846.9 90.0 %copy-start.1 = (bf16[688,1536]{1,0:T(8,128)(2,1)S(1)}, bf16[688,1536]{1,0:T(8,128)(2,1)}, u32[]{:S(2)}) copy-start(bf16[688,1536]{1,0:T(8,128)(2,1)} %param.7) | copy-start | bytes 6340612
Sparse Core Ops, SparseCore 0:
  9.6 246.6 all-gather.8
  272.4 148.8 all-gather.4
  422.9 148.9 all-gather.6
  655.1 116.2 all-reduce.3
  780.5 23.4 reduce-scatter.7
  847.0 43.7 reduce-scatter.5
  893.7 43.1 reduce-scatter.3
where the time goes:
time: 945 us; the launch traced here: 944 us
  waiting for transfers between devices  585 us (62%)
  matrix products  166 us (18%)
  other arithmetic  81.4 us (9%)
  blocking collectives  62 us (7%)
  local copies, waits for them, and re-layouts  33.9 us (4%)
  between operations  14.4 us (2%)
    all_gather x1, waiting for transfers between devices, body(): lax.all_gather(own_columns, 'dp', axis=1, tiled=True)  248 us
    all_gather x1, waiting for transfers between devices, body(): lax.all_gather(keys_local, 'dp', axis=0, tiled=True)  136 us
    psum x1, waiting for transfers between devices, body(): summed = lax.psum(context, 'member')  116 us
    reduce_sum x1, other arithmetic, body(): denom_sum = jnp.sum(expsc, axis=-1)  76.1 us
    dot_general x1, matrix products, body(): jnp.einsum('hqk,khd->qhd', expsc.astype(jnp.bfloat16), value_heads, prefe...  67 us
    dot_general x1, matrix products, body(): jnp.einsum('qhd,khd->hqk', queries, key_heads, preferred_element_type=jnp...  66.7 us
    psum x1, blocking collectives, body(): out_grad = lax.psum(out_part, 'member').astype(jnp.bfloat16)  62 us
    reduce_scatter x1, waiting for transfers between devices, body(): lax.psum_scatter(grad_up, 'dp', scatter_dimension=0, tiled=True)  46.2 us
  transfers between devices with their start and end apart: 7, of which 5 were waited for; matrix products, arithmetic and copies ran while one was open for 19% of the time, Pallas kernels for 0%

commit v1 on v0

--- a/solution.py
+++ b/solution.py
@@ -4,10 +4,167 @@
 import jax
 import jax.numpy as jnp
 from jax import lax
+from jax.experimental import pallas as pl
+from jax.experimental.pallas import tpu as pltpu
 from jax.sharding import PartitionSpec as P
 
 VALID = 1370
 IMAGES = 2
+HEAD = 64
+PAIR = 2 * HEAD
+ROWS = 16
+
+
+def attention_kernel(tile, q_ref, k_ref, v_ref, bias_ref, out_ref):
+    rows = q_ref.shape[1]
+    lane = lax.broadcasted_iota(jnp.int32, (rows, PAIR), 1)
+    keys, values = k_ref[0], v_ref[0]
+    bias = bias_ref[...]
+    sides = []
+    for head in range(2):
+        own = (lane < HEAD) if head == 0 else (lane >= HEAD)
+        sides.append((jnp.where(own, keys, bias), jnp.where(own, values, jnp.ones_like(values))))
+    tile_lane = lax.broadcasted_iota(jnp.int32, (tile, PAIR), 1)
+    for at in range(rows // tile):
+        queries = q_ref[0, at * tile : (at + 1) * tile, :] * jnp.asarray(0.125, jnp.bfloat16)
+        parts = []
+        for head in range(2):
+            own = (tile_lane < HEAD) if head == 0 else (tile_lane >= HEAD)
+            mark = jnp.where(tile_lane == (1 - head) * HEAD, 1.0, 0.0).astype(jnp.bfloat16)
+            scores = lax.dot_general(
+                jnp.where(own, queries, mark), sides[head][0], (((1,), (1,)), ((), ())),
+                preferred_element_type=jnp.float32,
+            )
+            top = jnp.max(scores, axis=-1, keepdims=True)
+            probs = jnp.exp(scores - top).astype(jnp.bfloat16)
+            mixed = jnp.dot(probs, sides[head][1], preferred_element_type=jnp.float32)
+            parts.append(mixed / pltpu.roll(mixed, HEAD, 1))
+        joined = jnp.where(tile_lane < HEAD, parts[0], parts[1])
+        out_ref[0, at * tile : (at + 1) * tile, :] = joined.astype(out_ref.dtype)
+
+
+def attention(projected, bias):
+    images, rows, width = projected.shape
+    pairs = width // 3 // PAIR
+    tile = rows // 4 if rows % (4 * ROWS) == 0 else rows
+    block = lambda first: pl.BlockSpec((1, rows, PAIR), lambda i, p: (i, 0, first + p))
+    return pl.pallas_call(
+        partial(attention_kernel, tile),
+        grid=(images, pairs),
+        in_specs=[block(0), block(pairs), block(2 * pairs), pl.BlockSpec((rows, PAIR), lambda i, p: (0, 0))],
+        out_specs=pl.BlockSpec((1, rows, PAIR), lambda i, p: (i, 0, p)),
+        out_shape=jax.ShapeDtypeStruct((images, rows, width // 3), jnp.bfloat16),
+        compiler_params=pltpu.CompilerParams(vmem_limit_bytes=48 * 1024 * 1024),
+        cost_estimate=pl.CostEstimate(
+            flops=images * pairs * 2 * rows * rows * PAIR * 4,
+            bytes_accessed=images * rows * width * 3,
+            transcendentals=images * pairs * 2 * rows * rows,
+        ),
+        name="attention",
+    )(projected, projected, projected, bias)
+
+
+def by_image(tokens, slot_rows):
+    rows, width = tokens.shape
+    split = tokens.reshape(rows // IMAGES, IMAGES, width).transpose(1, 0, 2)
+    return jnp.pad(split, ((0, 0), (0, slot_rows - rows // IMAGES), (0, 0)))
+
+
+def gather_teacher(tokens, weights, dp, member):
+    images, rows, width = tokens.shape
+    share = width * images // member
+    me = lax.axis_index("member")
+    block = lax.dynamic_slice(tokens, (me % images, 0, (me // images) * share), (1, rows, share))[0]
+    column = lax.all_gather(block, "dp", axis=0, tiled=True)
+    every = lax.all_gather(column, "member", axis=0, tiled=False)
+    every = every.reshape(member // images, images, dp * rows, share).transpose(1, 2, 0, 3)
+    every = every.reshape(images, dp * rows, width)
+    piece = weights.shape[1] // 3
+    came = []
+    for j in range(3):
+        pairs = [(s, (3 * s + j) % dp) for s in range(dp)]
+        came.append(lax.ppermute(weights[:, j * piece : (j + 1) * piece], "dp", pairs))
+    came = jnp.stack(came)
+    at = lax.axis_index("dp")
+    table = [[0] * 3 for _ in range(dp)]
+    for s in range(dp):
+        for j in range(3):
+            table[(3 * s + j) % dp][(3 * s + j) // dp] = j
+    order = jnp.asarray(table, jnp.int32)[at]
+    own = [lax.dynamic_index_in_dim(came, order[c], 0, keepdims=False) for c in range(3)]
+    return every, jnp.concatenate(own, axis=1)
+
+
+def split_body(dp, member, teacher_tokens, teacher_qkv, student_tokens, student_gain, w_up, w_down, w_head):
+    part_rows = teacher_tokens.shape[0] // IMAGES
+    slot_rows = -(-part_rows // ROWS) * ROWS
+    own_rows = IMAGES * slot_rows // member
+    quarter = slot_rows // own_rows
+    dp_at, member_at = lax.axis_index("dp"), lax.axis_index("member")
+
+    tokens, weights = gather_teacher(by_image(teacher_tokens, slot_rows), teacher_qkv[0], dp, member)
+
+    student = by_image(student_tokens, slot_rows).reshape(IMAGES * slot_rows, -1)
+    inputs = student.astype(jnp.float32)
+    in_mean = jnp.mean(inputs, axis=-1, keepdims=True)
+    in_var = jnp.mean((inputs - in_mean) ** 2, axis=-1, keepdims=True)
+    normed = ((inputs - in_mean) * lax.rsqrt(in_var + 1e-06) * student_gain).astype(jnp.bfloat16)
+    pre = jnp.dot(normed, w_up, preferred_element_type=jnp.float32)
+    gelu_tanh = partial(jax.nn.gelu, approximate=True)
+    hidden = gelu_tanh(pre).astype(jnp.bfloat16)
+    branch_part = lax.dot_general(
+        hidden, w_down, (((1,), (1,)), ((), ())), preferred_element_type=jnp.float32
+    )
+    branch = lax.psum_scatter(branch_part, "member", scatter_dimension=0, tiled=True)
+    own_inputs = lax.dynamic_slice_in_dim(student, member_at * own_rows, own_rows, 0).astype(jnp.float32)
+    own_out = (own_inputs + branch).astype(jnp.bfloat16)
+    student_out = lax.all_gather(own_out, "member", axis=0, tiled=True)
+    head_all = lax.all_gather(w_head, "member", axis=1, tiled=True)
+
+    images, rows, width = tokens.shape
+    projected = jnp.dot(
+        tokens.reshape(images * rows, width), weights, preferred_element_type=jnp.float32
+    ).astype(jnp.bfloat16).reshape(images, rows, -1)
+    key_row = jnp.arange(rows, dtype=jnp.int32)
+    in_part = key_row % slot_rows
+    real_key = (in_part < part_rows) & (key_row // slot_rows * part_rows + in_part < VALID)
+    bias = jnp.broadcast_to(jnp.where(real_key, 0.0, -1e30).astype(jnp.bfloat16)[:, None], (rows, PAIR))
+    context = attention(projected, bias)
+    share = context.shape[-1]
+    context = context.reshape(images, dp, quarter, own_rows, share).transpose(0, 2, 1, 3, 4)
+    context = context.reshape(member, dp * own_rows, share)
+    summed = lax.psum_scatter(context, "member", scatter_dimension=0, tiled=False)
+    summed = lax.all_to_all(summed.reshape(dp, own_rows, share), "dp", 0, 0, tiled=False)
+    summed = summed.transpose(1, 0, 2).reshape(own_rows, width).astype(jnp.float32)
+    row_mean = jnp.mean(summed, axis=-1, keepdims=True)
+    mean_square = jnp.mean(summed * summed, axis=-1, keepdims=True)
+    target = (summed - row_mean) * lax.rsqrt(mean_square - row_mean * row_mean + 1e-06)
+
+    own_row = (member_at % quarter) * own_rows + jnp.arange(own_rows, dtype=jnp.int32)
+    real = (own_row < part_rows) & (dp_at * part_rows + own_row < VALID)
+    pred = jnp.dot(own_out, head_all, preferred_element_type=jnp.float32)
+    own_grad = jnp.where(real[:, None], (pred - target) / math.sqrt(IMAGES * VALID), 0.0).astype(jnp.bfloat16)
+    pred_grad = lax.all_gather(own_grad, "member", axis=0, tiled=True)
+    head_width = w_head.shape[1]
+    own_columns = lax.dynamic_slice_in_dim(pred_grad, member_at * head_width, head_width, 1)
+    out_grad = lax.dot_general(
+        pred_grad, head_all, (((1,), (1,)), ((), ())), preferred_element_type=jnp.float32
+    ).astype(jnp.bfloat16)
+    grad_down = lax.dot_general(
+        out_grad, hidden, (((0,), (0,)), ((), ())), preferred_element_type=jnp.float32
+    )
+    hidden_grad = jnp.dot(out_grad, w_down, preferred_element_type=jnp.float32)
+    _, pullback = jax.vjp(gelu_tanh, pre)
+    pre_grad = pullback(hidden_grad)[0].astype(jnp.bfloat16)
+    grad_up = lax.dot_general(
+        normed, pre_grad, (((0,), (0,)), ((), ())), preferred_element_type=jnp.float32
+    )
+    grad_head = lax.dot_general(
+        student_out, own_columns, (((0,), (0,)), ((), ())), preferred_element_type=jnp.float32
+    )
+    return tuple(
+        lax.psum_scatter(g, "dp", scatter_dimension=0, tiled=True) for g in (grad_up, grad_down, grad_head)
+    )
 
 
 def body(teacher_tokens, teacher_qkv, student_tokens, student_gain, w_up, w_down, w_head):
@@ -94,6 +251,17 @@
     return (grad_up, grad_down, grad_head)
 
 
+def can_split(dp, member, tokens, feat):
+    slot_rows = -(-(tokens // dp // IMAGES) // ROWS) * ROWS
+    return (
+        math.gcd(3, dp) == 1
+        and feat % (dp * PAIR) == 0
+        and member % IMAGES == 0
+        and (feat * IMAGES) % (member * PAIR) == 0
+        and slot_rows * IMAGES % (member * 8) == 0
+    )
+
+
 def solution(mesh):
     in_specs = (
         P("dp", None),
@@ -105,4 +273,13 @@
         P(None, "member"),
     )
     out_specs = (P("dp", "member"), P("dp", "member"), P("dp", "member"))
-    return jax.shard_map(body, mesh=mesh, in_specs=in_specs, out_specs=out_specs, check_vma=False)
+
+    def run(teacher_tokens, *rest):
+        dp, member = mesh.shape["dp"], mesh.shape["member"]
+        part = body
+        if can_split(dp, member, *teacher_tokens.shape):
+            part = partial(split_body, dp, member)
+        call = jax.shard_map(part, mesh=mesh, in_specs=in_specs, out_specs=out_specs, check_vma=False)
+        return call(teacher_tokens, *rest)
+
+    return run

time: 945 us -> 469 us (0.50)
  waiting for transfers between devices: 585 us -> 286 us
  matrix products: 166 us -> 39.3 us
  other arithmetic: 81.4 us -> 5.75 us
  blocking collectives: 62 us -> 0 us
  Pallas kernels: 0 us -> 39.6 us
  local copies, waits for them, and re-layouts: 33.9 us -> 57.6 us
  starting transfers between devices: 0.69 us -> 19.4 us
    all_gather x3 -> x5, waiting for transfers between devices: 385 us -> 106 us  [the longest x1 31.3 us: gather_teacher(): column = lax.all_gather(block, 'dp', axis=0, tiled=True)]
    dot_general x10 -> x8, matrix products: 166 us -> 39.3 us  [the longest x1 15.9 us: split_body(): jnp.dot(tokens.reshape(images * rows, width), weights, preferred_element_...]
    psum x1 -> x0, waiting for transfers between devices: 116 us -> none  [body(): summed = lax.psum(context, 'member')]
    reduce_sum x4 -> x3, other arithmetic: 79.9 us -> 0.94 us  [the longest x1 0.52 us: split_body(): in_var = jnp.mean((inputs - in_mean) ** 2, axis=-1, keepdims=True)]
    psum x1 -> x0, blocking collectives: 62 us -> none  [body(): out_grad = lax.psum(out_part, 'member').astype(jnp.bfloat16)]
    reduce_scatter x3 -> x5, waiting for transfers between devices: 84 us -> 140 us  [the longest x3 101 us: split_body(): lax.psum_scatter(g, 'dp', scatter_dimension=0, tiled=True)]
    pallas_call x0 -> x1, Pallas kernels: none -> 39.6 us  [attention(): pl.pallas_call(partial(attention_kernel, tile), grid=(images, pairs), in_...]
    ppermute x0 -> x3, waiting for transfers between devices: none -> 30.8 us  [gather_teacher(): lax.ppermute(weights[:, j * piece:(j + 1) * piece], 'dp', pairs)]
  transfers between devices with their start and end apart: 7 -> 14, of which waited for: 5 -> 10; matrix products, arithmetic and copies ran while one was open for 19% -> 19% of each run, Pallas kernels for 0% -> 8%
where the time goes in v1:
time: 469 us; the launch traced here: 468 us
  waiting for transfers between devices  286 us (61%)
  local copies, waits for them, and re-layouts  57.6 us (12%)
  Pallas kernels  39.6 us (8%)
  matrix products  39.3 us (8%)
  between operations  20.2 us (4%)
  starting transfers between devices  19.4 us (4%)
  other arithmetic  5.75 us (1%)
    reduce_scatter x3, waiting for transfers between devices, split_body(): lax.psum_scatter(g, 'dp', scatter_dimension=0, tiled=True)  101 us
    pallas_call x1, Pallas kernels, attention(): pl.pallas_call(partial(attention_kernel, tile), grid=(images, pairs), in_...  39.6 us
    reduce_scatter x1, waiting for transfers between devices, split_body(): lax.psum_scatter(context, 'member', scatter_dimension=0, tiled=False)  38.4 us
    all_gather x1, waiting for transfers between devices, gather_teacher(): column = lax.all_gather(block, 'dp', axis=0, tiled=True)  31.3 us
    ppermute x3, waiting for transfers between devices, gather_teacher(): lax.ppermute(weights[:, j * piece:(j + 1) * piece], 'dp', pairs)  30.8 us
    all_gather x1, waiting for transfers between devices, split_body(): pred_grad = lax.all_gather(own_grad, 'member', axis=0, tiled=True)  30.7 us
    transpose x1, local copies, waits for them, and re-layouts, gather_teacher(): every.reshape(member // images, images, dp * rows, share)  26.3 us
    all_gather x1, waiting for transfers between devices, split_body(): student_out = lax.all_gather(own_out, 'member', axis=0, tiled=True)  23.7 us
  transfers between devices with their start and end apart: 14, of which 10 were waited for; matrix products, arithmetic and copies ran while one was open for 19% of the time, Pallas kernels for 8%

profile of v1, /device:TPU:0, one launch (start us, length us, event | category | flops | bytes accessed | tf_op | source)
XLA Modules:
  0.0 467.7 jit_solution(17838240654650237602)
XLA Ops:
  7.3 4.4 reshape.121
  13.6 31.3 %all-gather.14.cloned.1.call-done = bf16[1,1408,384]{2,1,0:T(8,128)(2,1)} async-done(((bf16[1,352,384]{2,1,0:T(8,128)(2,1)}), bf16[1,1408,384]{2,1,0:T(8,128)(2,1)}) %all-gather.14.cloned.1.call-update) | async-done | bytes 1081360 | tf_op jit(solution)/shard_map/all_gather | solution.py:78
  45.0 4.1 fusion.44
  49.0 10.4 %collective-permute-start = (bf16[1536,384]{1,0:T(8,128)(2,1)}, bf16[1536,384]{1,0:T(8,128)(2,1)}, u32[]{:S(2)}, u32[]{:S(2)}) collective-permute-start(bf16[1536,384]{1,0:T(8,128)(2,1)} %get-tuple-element.8), channel_id=1, source_target_pairs={{0,0},{1,3},{2,2},{3,1},{4,4},{5,7},{6,6},{7,5},{8,8},{9,11},{10,1... | collective-permute-start | bytes 3538952 | tf_op jit(solution)/shard_map/ppermute | solution.py:86
  59.5 3.8 collective-permute-start.2
  63.3 1.4 reshape.119
  64.7 1.7 copy.32
  71.8 2.6 fusion.43
  81.8 30.8 %collective-permute-done.1 = bf16[1536,384]{1,0:T(8,128)(2,1)} collective-permute-done((bf16[1536,384]{1,0:T(8,128)(2,1)}, bf16[1536,384]{1,0:T(8,128)(2,1)}, u32[]{:S(2)}, u32[]{:S(2)}) %collective-permute-start.1) | collective-permute-done | bytes 1179680 | tf_op jit(solution)/shard_map/ppermute | solution.py:86
  112.6 2.5 pad_maximum_fusion
  115.1 1.9 dynamic-slice_bitcast_fusion.2
  117.0 26.3 %copy.26 = bf16[2,1408,4,384]{3,2,1,0:T(4,128)(2,1)} copy(bf16[2,1408,4,384]{3,1,0,2:T(8,128)(2,1)} %bitcast.53) | data formatting | bytes 17301504 | tf_op jit(solution)/shard_map/transpose | solution.py:80
  143.3 8.5 %copy.30 = bf16[352,8,4,384]{3,1,2,0:T(8,128)(2,1)} copy(bf16[352,8,4,384]{3,2,1,0:T(4,128)(2,1)} %bitcast.49) | data formatting | bytes 17301504
  151.8 15.9 %convolution_convert_fusion = bf16[2816,1152]{1,0:T(8,128)(2,1)} fusion(bf16[2816,1536]{1,0:T(8,128)(2,1)} %bitcast.54, bf16[1536,384]{1,0:T(8,128)(2,1)S(1)} %copy-done.5, bf16[1536,384]{1,0:T(8,128)(2,1)} %get-tuple-element.7, bf16[1536,384]{1,0:T(8,128)(2,1)S(1)} %copy-done.4), kind=kOutput, calls=%fused_computation | convolution fusion | flops 9979527168 | bytes 18677760 | tf_op jit(solution)/shard_map/dot_general | solution.py:125
  168.0 39.6 %attention.1 = bf16[2,1408,384]{2,1,0:T(8,128)(2,1)S(1)} custom-call(bf16[2,1408,1152]{2,1,0:T(8,128)(2,1)} %bitcast.61, bf16[2,1408,1152]{2,1,0:T(8,128)(2,1)} %bitcast.62, bf16[2,1408,1152]{2,1,0:T(8,128)(2,1)} %bitcast.63, bf16[1408,128]{1,0:T(8,128)(2,1)S(1)} %broadcast_in_dim.35.bias_ref), custom_call_target="tpu_custom_call" | custom-call | flops 12180258816 | bytes 9732096 | tf_op jit(solution)/shard_map/attention/pallas_call | solution.py:51
  207.6 1.6 copy.27
  209.9 1.7 add_convert_fusion
  211.7 38.4 %reduce-scatter.8.cloned.1.call-done = bf16[1,352,384]{2,1,0:T(8,128)(2,1)} async-done(((bf16[8,352,384]{2,1,0:T(8,128)(2,1)}), bf16[1,352,384]{2,1,0:T(8,128)(2,1)}) %reduce-scatter.8.cloned.1.call-update) | async-done | bytes 270352 | tf_op jit(solution)/shard_map/reduce_scatter | solution.py:136
  250.0 4.6 all-to-all-start
  254.7 9.1 %all-to-all-done = bf16[4,88,384]{2,1,0:T(8,128)(2,1)S(1)} async-done(((bf16[4,88,384]{2,1,0:T(8,128)(2,1)}), bf16[4,88,384]{2,1,0:T(8,128)(2,1)S(1)}, u32[]{:S(2)}, u32[]{:S(2)}) %all-to-all-start) | async-done | bytes 270368 | tf_op jit(solution)/shard_map/all_to_all | solution.py:137
  264.0 20.1 %all-gather.8.cloned.1.call-done = bf16[1024,1536]{0,1:T(8,128)(2,1)} async-done(((bf16[1024,192]{0,1:T(8,128)(2,1)}), bf16[1024,1536]{0,1:T(8,128)(2,1)}) %all-gather.8.cloned.1.call-update) | async-done | bytes 3145744 | tf_op jit(solution)/shard_map/all_gather | solution.py:122
  284.1 3.7 fusion.9
  287.9 23.7 %all-gather.12.cloned.1.call-done = bf16[704,1024]{1,0:T(8,128)(2,1)} async-done(((bf16[88,1024]{1,0:T(8,128)(2,1)}), bf16[704,1024]{1,0:T(8,128)(2,1)}) %all-gather.12.cloned.1.call-update) | async-done | bytes 1441808 | tf_op jit(solution)/shard_map/all_gather | solution.py:121
  311.6 30.7 %all-gather.10.cloned.1.call-done = bf16[704,1536]{1,0:T(8,128)(2,1)} async-done(((bf16[88,1536]{1,0:T(8,128)(2,1)}), bf16[704,1536]{1,0:T(8,128)(2,1)}) %all-gather.10.cloned.1.call-update) | async-done | bytes 2162704 | tf_op jit(solution)/shard_map/all_gather | solution.py:147
  342.3 3.1 fusion.20
  345.5 5.0 %convolution_convert_fusion.1 = bf16[704,1024]{1,0:T(8,128)(2,1)S(1)} fusion(bf16[704,1536]{1,0:T(8,128)(2,1)} %all-gather.10.cloned.1.call-done, bf16[1024,1536]{0,1:T(8,128)(2,1)} %all-gather.8.cloned.1.call-done), kind=kOutput, calls=%fused_computation.19 | convolution fusion | flops 2215313408 | bytes 6750208 | tf_op jit(solution)/shard_map/dot_general | solution.py:150
  350.5 1.1 copy-done.10
  351.7 2.5 fusion.42
  354.2 5.6 %fusion.17 = f32[1024,512]{1,0:T(8,128)} fusion(bf16[704,1024]{1,0:T(8,128)(2,1)S(1)} %multiply_convert_fusion, f32[704,512]{1,0:T(8,128)} %copy-done.8, bf16[704,1024]{1,0:T(8,128)(2,1)} %copy-done.10, bf16[1024,512]{1,0:T(8,128)(2,1)S(1)} %copy-done), kind=kOutput, calls=%fused_computation.35 | convolution fusion | flops 1483603968 | bytes 7471104 | tf_op jit(solution)/shard_map/dot_general | solution.py:159
  359.8 9.1 %reduce-scatter.14.cloned.1.call-done = f32[256,192]{0,1:T(8,128)} async-done(((f32[1024,192]{0,1:T(8,128)}), f32[256,192]{0,1:T(8,128)}) %reduce-scatter.14.cloned.1.call-update) | async-done | bytes 196624 | tf_op jit(solution)/shard_map/reduce_scatter | solution.py:166
  368.9 46.0 %reduce-scatter.12.cloned.1.call-done = f32[256,512]{1,0:T(8,128)} async-done(((f32[1024,512]{1,0:T(8,128)}), f32[256,512]{1,0:T(8,128)}) %reduce-scatter.12.cloned.1.call-update) | async-done | bytes 524304 | tf_op jit(solution)/shard_map/reduce_scatter | solution.py:166
  414.9 46.0 %reduce-scatter.10.cloned.1.call-done = f32[256,512]{1,0:T(8,128)} async-done(((f32[1024,512]{1,0:T(8,128)}), f32[256,512]{1,0:T(8,128)}) %reduce-scatter.10.cloned.1.call-update) | async-done | bytes 524304 | tf_op jit(solution)/shard_map/reduce_scatter | solution.py:166
  (66 shorter events, 10.3 us)
Async XLA Ops:
  7.2 64.7 %copy-start = (bf16[1024,512]{1,0:T(8,128)(2,1)S(1)}, bf16[1024,512]{1,0:T(8,128)(2,1)}, u32[]{:S(2)}) copy-start(bf16[1024,512]{1,0:T(8,128)(2,1)} %param.13) | copy-start | bytes 3145732
  7.2 37.7 %all-gather.14.cloned.1.call-start = ((), (), s32[]{:S(2)}) async-start(), calls=%async_computation.14 | async-start | bytes 1351680 | tf_op jit(solution)/shard_map/all_gather | solution.py:78
  13.5 103.5 %all-gather.16.cloned.1.call-start = ((), (), s32[]{:S(2)}) async-start(), calls=%async_computation.15 | async-start | bytes 9732096 | tf_op jit(solution)/shard_map/all_gather | solution.py:79
  44.9 165.0 %reduce-scatter.6.cloned.1.call-start = ((), (), s32[]{:S(2)}) async-start(), calls=%async_computation.6 | async-start | bytes 3244032 | tf_op jit(solution)/shard_map/reduce_scatter | solution.py:118
  44.9 18.4 %copy-start.3 = (bf16[688,1024]{1,0:T(8,128)(2,1)S(1)}, bf16[688,1024]{1,0:T(8,128)(2,1)}, u32[]{:S(2)}) copy-start(bf16[688,1024]{1,0:T(8,128)(2,1)} %param.10) | copy-start | bytes 4227076
  49.0 32.7 %collective-permute-start = (bf16[1536,384]{1,0:T(8,128)(2,1)}, bf16[1536,384]{1,0:T(8,128)(2,1)}, u32[]{:S(2)}, u32[]{:S(2)}) collective-permute-start(bf16[1536,384]{1,0:T(8,128)(2,1)} %get-tuple-element.8), channel_id=1, source_target_pairs={{0,0},{1,3},{2,2},{3,1},{4,4},{5,7},{6,6},{7,5},{8,8},{9,11},{10,1... | collective-permute-start | bytes 3538952 | tf_op jit(solution)/shard_map/ppermute | solution.py:86
  59.5 53.1 %collective-permute-start.1 = (bf16[1536,384]{1,0:T(8,128)(2,1)}, bf16[1536,384]{1,0:T(8,128)(2,1)}, u32[]{:S(2)}, u32[]{:S(2)}) collective-permute-start(bf16[1536,384]{1,0:T(8,128)(2,1)} %get-tuple-element.10), channel_id=1, source_target_pairs={{0,1},{1,0},{2,3},{3,2},{4,5},{5,4},{6,7},{7,6},{8,9},{9,8},{10,11... | collective-permute-start | bytes 3538952 | tf_op jit(solution)/shard_map/ppermute | solution.py:86
  59.5 53.1 %collective-permute-start.2 = (bf16[1536,384]{1,0:T(8,128)(2,1)}, bf16[1536,384]{1,0:T(8,128)(2,1)}, u32[]{:S(2)}, u32[]{:S(2)}) collective-permute-start(bf16[1536,384]{1,0:T(8,128)(2,1)} %get-tuple-element.9), channel_id=1, source_target_pairs={{0,2},{1,1},{2,0},{3,3},{4,6},{5,5},{6,4},{7,7},{8,10},{9,9},{10,8... | collective-permute-start | bytes 3538952 | tf_op jit(solution)/shard_map/ppermute | solution.py:86
  67.3 0.7 copy-start.6
  68.0 1.1 copy-start.1
  68.0 1.7 copy-start.7
  70.7 1.1 copy-start.8
  74.4 175.6 %reduce-scatter.8.cloned.1.call-start = ((), (), s32[]{:S(2)}) async-start(), calls=%async_computation.8 | async-start | bytes 2433024 | tf_op jit(solution)/shard_map/reduce_scatter | solution.py:136
  143.3 8.5 %copy-start.4 = (bf16[1536,384]{1,0:T(8,128)(2,1)S(1)}, bf16[1536,384]{1,0:T(8,128)(2,1)}, u32[]{:S(2)}) copy-start(bf16[1536,384]{1,0:T(8,128)(2,1)} %get-tuple-element.5) | copy-start | bytes 3538948
  143.3 8.5 %copy-start.5 = (bf16[1536,384]{1,0:T(8,128)(2,1)S(1)}, bf16[1536,384]{1,0:T(8,128)(2,1)}, u32[]{:S(2)}) copy-start(bf16[1536,384]{1,0:T(8,128)(2,1)} %get-tuple-element.6) | copy-start | bytes 3538948
  209.2 74.9 %all-gather.8.cloned.1.call-start = ((), (), s32[]{:S(2)}) async-start(), calls=%async_computation.7 | async-start | bytes 3538944 | tf_op jit(solution)/shard_map/all_gather | solution.py:122
  209.8 101.8 %all-gather.12.cloned.1.call-start = ((), (), s32[]{:S(2)}) async-start(), calls=%async_computation.12 | async-start | bytes 1622016 | tf_op jit(solution)/shard_map/all_gather | solution.py:121
  211.6 72.5 %copy-start.2 = (bf16[88,1024]{1,0:T(8,128)(2,1)S(1)}, bf16[88,1024]{1,0:T(8,128)(2,1)}, u32[]{:S(2)}) copy-start(bf16[88,1024]{1,0:T(8,128)(2,1)} %add_convert_fusion) | copy-start | bytes 540676
  250.0 13.7 %all-to-all-start = ((bf16[4,88,384]{2,1,0:T(8,128)(2,1)}), bf16[4,88,384]{2,1,0:T(8,128)(2,1)S(1)}, u32[]{:S(2)}, u32[]{:S(2)}) async-start(bf16[4,88,384]{2,1,0:T(8,128)(2,1)} %bitcast.60), calls=%async_computation.2 | async-start | bytes 540672 | tf_op jit(solution)/shard_map/all_to_all | solution.py:137
  254.6 87.6 %all-gather.10.cloned.1.call-start = ((), (), s32[]{:S(2)}) async-start(), calls=%async_computation.9 | async-start | bytes 2433024 | tf_op jit(solution)/shard_map/all_gather | solution.py:147
  287.8 81.0 %reduce-scatter.14.cloned.1.call-start = ((), (), s32[]{:S(2)}) async-start(), calls=%async_computation.13 | async-start | bytes 983040 | tf_op jit(solution)/shard_map/reduce_scatter | solution.py:166
  345.4 69.5 %reduce-scatter.12.cloned.1.call-start = ((), (), s32[]{:S(2)}) async-start(), calls=%async_computation.11 | async-start | bytes 2621440 | tf_op jit(solution)/shard_map/reduce_scatter | solution.py:166
  345.5 6.2 %copy-start.9 = (f32[704,512]{1,0:T(8,128)S(1)}, f32[704,512]{1,0:T(8,128)}, u32[]{:S(2)}) copy-start(f32[704,512]{1,0:T(8,128)} %copy-done.8) | copy-start | bytes 4325380
  350.5 1.1 copy-start.10
  354.1 106.8 %reduce-scatter.10.cloned.1.call-start = ((), (), s32[]{:S(2)}) async-start(), calls=%async_computation.10 | async-start | bytes 2621440 | tf_op jit(solution)/shard_map/reduce_scatter | solution.py:166
Sparse Core Ops, SparseCore 0:
  13.7 31.1 all-gather.13
  46.8 54.9 all-gather.15
  105.2 44.9 reduce-scatter.5
  209.3 40.6 reduce-scatter.7
  251.8 32.2 all-gather.7
  286.4 25.1 all-gather.11
  314.1 28.1 all-gather.9
  345.5 23.2 reduce-scatter.13
  371.7 43.1 reduce-scatter.11
  417.7 43.1 reduce-scatter.9

commit v2 on v1

--- a/solution.py
+++ b/solution.py
@@ -70,29 +70,139 @@
     return jnp.pad(split, ((0, 0), (0, slot_rows - rows // IMAGES), (0, 0)))
 
 
-def gather_teacher(tokens, weights, dp, member):
+def gather_kernel(dp, src, wts, tok, own, z_send, z_recv, p_send, p_recv, f_send, f_recv, w_send, w_recv, local):
+    rows, width = src.shape[1], src.shape[2]
+    depth, piece = wts.shape[0], wts.shape[1] // 3
+    m, z = lax.axis_index("member"), lax.axis_index("dp")
+    core, x, y = m % 2, (m // 2) % 2, m // 4
+    chips = 4
+    share = width // chips
+    other_core = m + 1 - 2 * core
+    to_x, to_y = 2 - 4 * x, 4 - 8 * y
+    peers = [m + to_x, m + to_y, m + to_x + to_y, other_core]
+
+    barrier = pltpu.get_barrier_semaphore()
+    for k in range(1, dp):
+        pl.semaphore_signal(
+            barrier, inc=1, device_id={"member": m, "dp": (z + k) % dp}, device_id_type=pl.DeviceIdType.MESH
+        )
+    for peer in peers:
+        pl.semaphore_signal(
+            barrier, inc=1, device_id={"member": peer, "dp": z}, device_id_type=pl.DeviceIdType.MESH
+        )
+    pl.semaphore_wait(barrier, dp - 1 + len(peers))
+
+    def columns(chip):
+        return pl.ds(pl.multiple_of(chip * share, PAIR), share)
+
+    def region(image, part, chip):
+        return tok.at[image, pl.ds(pl.multiple_of(part * rows, ROWS), rows), columns(chip)]
+
+    def send(source, target, sems, member, part):
+        return pltpu.make_async_remote_copy(
+            src_ref=source, dst_ref=target, send_sem=sems[0], recv_sem=sems[1],
+            device_id={"member": member, "dp": part}, device_id_type=pl.DeviceIdType.MESH,
+        )
+
+    chip = m // 2
+    first = []
+    for k in range(1, dp):
+        copy = send(
+            src.at[core, :, columns(chip)], region(core, z, chip),
+            (z_send.at[k - 1], z_recv.at[k - 1]), m, (z + k) % dp,
+        )
+        copy.start()
+        first.append(copy)
+    stay = pltpu.make_async_copy(src, tok.at[:, pl.ds(pl.multiple_of(z * rows, ROWS), rows), :], local.at[3])
+    stay.start()
+
+    def weight_copy(j):
+        dest, slot = (3 * z + j) % dp, (3 * z + j) // dp
+        source = wts.at[:, pl.ds(j * piece, piece)]
+        target = own.at[:, pl.ds(pl.multiple_of(slot * piece, PAIR), piece)]
+        return dest, source, target, slot
+
+    for j in range(3):
+        dest, source, target, slot = weight_copy(j)
+
+        @pl.when(dest == z)
+        def _():
+            pltpu.make_async_copy(source, target, local.at[j]).start()
+
+        @pl.when(dest != z)
+        def _():
+            send(source, target, (w_send.at[j], w_recv.at[slot]), m, dest).start()
+
+    passed = []
+    for k in range(1, dp):
+        part = (z + dp - k) % dp
+        here = region(core, part, chip)
+        first[k - 1].wait_recv()
+        for p, peer in enumerate(peers):
+            copy = send(here, here, (p_send.at[k - 1, p], p_recv.at[k - 1, p]), peer, z)
+            copy.start()
+            passed.append(copy)
+    chips_of = [(m + to_x) // 2, (m + to_y) // 2, (m + to_x + to_y) // 2]
+    for k in range(1, dp):
+        part = (z + dp - k) % dp
+        for p in range(3):
+            here = region(core, part, chips_of[p])
+            send(here, here, (p_send.at[k - 1, p], p_recv.at[k - 1, p]), other_core, z).wait_recv()
+            copy = send(here, here, (f_send.at[k - 1, p], f_recv.at[k - 1, p]), other_core, z)
+            copy.start()
+            passed.append(copy)
+    for k in range(1, dp):
+        part = (z + dp - k) % dp
+        there = region(1 - core, part, chip)
+        send(there, there, (p_send.at[k - 1, 3], p_recv.at[k - 1, 3]), other_core, z).wait_recv()
+        for p in range(3):
+            there = region(1 - core, part, chips_of[p])
+            send(there, there, (f_send.at[k - 1, p], f_recv.at[k - 1, p]), other_core, z).wait_recv()
+    for copy in first + passed:
+        copy.wait_send()
+    for j in range(3):
+        dest, source, target, slot = weight_copy(j)
+
+        @pl.when(dest == z)
+        def _():
+            pltpu.make_async_copy(source, target, local.at[j]).wait()
+
+        @pl.when(dest != z)
+        def _():
+            send(source, target, (w_send.at[j], w_recv.at[slot]), m, dest).wait_send()
+
+    for slot in range(3):
+        place = own.at[:, pl.ds(slot * piece, piece)]
+
+        @pl.when((slot * dp + z) // 3 != z)
+        def _():
+            send(place, place, (w_send.at[0], w_recv.at[slot]), m, (z + 1) % dp).wait_recv()
+
+    stay.wait()
+
+
+def gather_teacher(tokens, weights, dp):
     images, rows, width = tokens.shape
-    share = width * images // member
-    me = lax.axis_index("member")
-    block = lax.dynamic_slice(tokens, (me % images, 0, (me // images) * share), (1, rows, share))[0]
-    column = lax.all_gather(block, "dp", axis=0, tiled=True)
-    every = lax.all_gather(column, "member", axis=0, tiled=False)
-    every = every.reshape(member // images, images, dp * rows, share).transpose(1, 2, 0, 3)
-    every = every.reshape(images, dp * rows, width)
-    piece = weights.shape[1] // 3
-    came = []
-    for j in range(3):
-        pairs = [(s, (3 * s + j) % dp) for s in range(dp)]
-        came.append(lax.ppermute(weights[:, j * piece : (j + 1) * piece], "dp", pairs))
-    came = jnp.stack(came)
-    at = lax.axis_index("dp")
-    table = [[0] * 3 for _ in range(dp)]
-    for s in range(dp):
-        for j in range(3):
-            table[(3 * s + j) % dp][(3 * s + j) // dp] = j
-    order = jnp.asarray(table, jnp.int32)[at]
-    own = [lax.dynamic_index_in_dim(came, order[c], 0, keepdims=False) for c in range(3)]
-    return every, jnp.concatenate(own, axis=1)
+    steps = dp - 1
+    dma = pltpu.SemaphoreType.DMA
+    return pl.pallas_call(
+        partial(gather_kernel, dp),
+        out_shape=(
+            jax.ShapeDtypeStruct((images, dp * rows, width), tokens.dtype),
+            jax.ShapeDtypeStruct(weights.shape, weights.dtype),
+        ),
+        in_specs=[pl.BlockSpec(memory_space=pl.ANY)] * 2,
+        out_specs=(pl.BlockSpec(memory_space=pl.ANY),) * 2,
+        scratch_shapes=[
+            dma((steps,)), dma((steps,)), dma((steps, 4)), dma((steps, 4)), dma((steps, 3)), dma((steps, 3)),
+            dma((3,)), dma((3,)), dma((4,)),
+        ],
+        compiler_params=pltpu.CompilerParams(collective_id=0, has_side_effects=True),
+        cost_estimate=pl.CostEstimate(
+            flops=0, bytes_accessed=64 * images * dp * rows * width, transcendentals=0
+        ),
+        name="gather_teacher",
+    )(tokens, weights)
 
 
 def split_body(dp, member, teacher_tokens, teacher_qkv, student_tokens, student_gain, w_up, w_down, w_head):
@@ -101,8 +211,6 @@
     own_rows = IMAGES * slot_rows // member
     quarter = slot_rows // own_rows
     dp_at, member_at = lax.axis_index("dp"), lax.axis_index("member")
-
-    tokens, weights = gather_teacher(by_image(teacher_tokens, slot_rows), teacher_qkv[0], dp, member)
 
     student = by_image(student_tokens, slot_rows).reshape(IMAGES * slot_rows, -1)
     inputs = student.astype(jnp.float32)
@@ -115,10 +223,11 @@
     branch_part = lax.dot_general(
         hidden, w_down, (((1,), (1,)), ((), ())), preferred_element_type=jnp.float32
     )
+    teacher_slots, branch_part = lax.optimization_barrier((by_image(teacher_tokens, slot_rows), branch_part))
+    tokens, weights = gather_teacher(teacher_slots, teacher_qkv[0], dp)
     branch = lax.psum_scatter(branch_part, "member", scatter_dimension=0, tiled=True)
     own_inputs = lax.dynamic_slice_in_dim(student, member_at * own_rows, own_rows, 0).astype(jnp.float32)
     own_out = (own_inputs + branch).astype(jnp.bfloat16)
-    student_out = lax.all_gather(own_out, "member", axis=0, tiled=True)
     head_all = lax.all_gather(w_head, "member", axis=1, tiled=True)
 
     images, rows, width = tokens.shape
@@ -129,6 +238,8 @@
     in_part = key_row % slot_rows
     real_key = (in_part < part_rows) & (key_row // slot_rows * part_rows + in_part < VALID)
     bias = jnp.broadcast_to(jnp.where(real_key, 0.0, -1e30).astype(jnp.bfloat16)[:, None], (rows, PAIR))
+    projected, student_out_own = lax.optimization_barrier((projected, own_out))
+    student_out = lax.all_gather(student_out_own, "member", axis=0, tiled=True)
     context = attention(projected, bias)
     share = context.shape[-1]
     context = context.reshape(images, dp, quarter, own_rows, share).transpose(0, 2, 1, 3, 4)
@@ -163,7 +274,8 @@
         student_out, own_columns, (((0,), (0,)), ((), ())), preferred_element_type=jnp.float32
     )
     return tuple(
-        lax.psum_scatter(g, "dp", scatter_dimension=0, tiled=True) for g in (grad_up, grad_down, grad_head)
+        lax.psum_scatter(g.astype(jnp.bfloat16), "dp", scatter_dimension=0, tiled=True).astype(jnp.float32)
+        for g in (grad_up, grad_down, grad_head)
     )
 
 
@@ -256,8 +368,8 @@
     return (
         math.gcd(3, dp) == 1
         and feat % (dp * PAIR) == 0
-        and member % IMAGES == 0
-        and (feat * IMAGES) % (member * PAIR) == 0
+        and member == 4 * IMAGES
+        and feat % (4 * PAIR) == 0
         and slot_rows * IMAGES % (member * 8) == 0
     )
 

time: 469 us -> 417 us (0.89)
  Pallas kernels: 39.6 us -> 147 us
  waiting for transfers between devices: 286 us -> 184 us
  local copies, waits for them, and re-layouts: 57.6 us -> 19 us
  starting transfers between devices: 19.4 us -> 5.29 us
  between operations: 20.2 us -> 14.3 us
    pallas_call x0 -> x1, Pallas kernels: none -> 108 us  [gather_teacher(): pl.pallas_call(partial(gather_kernel, dp), out_shape=(jax.ShapeDtypeStruc...]
    reduce_scatter x3, waiting for transfers between devices: 101 us -> 60.3 us  [split_body(): lax.psum_scatter(g.astype(jnp.bfloat16), 'dp', scatter_dimension=0, tiled...]
    all_gather x3 -> x1, waiting for transfers between devices: 55 us -> 23.7 us  [split_body(): student_out = lax.all_gather(student_out_own, 'member', axis=0, tiled=True)]
    ppermute x3 -> x0, waiting for transfers between devices: 30.8 us -> none  [gather_teacher(): lax.ppermute(weights[:, j * piece:(j + 1) * piece], 'dp', pairs)]
    transpose x1 -> x0, local copies, waits for them, and re-layouts: 26.3 us -> none  [gather_teacher(): every.reshape(member // images, images, dp * rows, share)]
    ppermute x3 -> x0, starting transfers between devices: 14.2 us -> none  [gather_teacher(): lax.ppermute(weights[:, j * piece:(j + 1) * piece], 'dp', pairs)]
    unnamed x23 -> x22, local copies, waits for them, and re-layouts: 12.5 us -> 3.64 us
    convert_element_type x0 -> x3, other arithmetic: none -> 5.19 us  [split_body(): lax.psum_scatter(g.astype(jnp.bfloat16), 'dp', scatter_dimension=0, tiled...]
  transfers between devices with their start and end apart: 14 -> 9, of which waited for: 10 -> 8; matrix products, arithmetic and copies ran while one was open for 19% -> 9% of each run, Pallas kernels for 8% -> 26%
where the time goes in v2:
time: 417 us
  waiting for transfers between devices  184 us (44%)
  Pallas kernels  147 us (35%)
  matrix products  38.6 us (9%)
  local copies, waits for them, and re-layouts  19 us (5%)
  between operations  14.3 us (3%)
  other arithmetic  8.39 us (2%)
  starting transfers between devices  5.29 us (1%)
    pallas_call x1, Pallas kernels, gather_teacher(): pl.pallas_call(partial(gather_kernel, dp), out_shape=(jax.ShapeDtypeStruc...  108 us
    reduce_scatter x3, waiting for transfers between devices, split_body(): lax.psum_scatter(g.astype(jnp.bfloat16), 'dp', scatter_dimension=0, tiled...  60.3 us
    pallas_call x1, Pallas kernels, attention(): pl.pallas_call(partial(attention_kernel, tile), grid=(images, pairs), in_...  39.3 us
    reduce_scatter x1, waiting for transfers between devices, split_body(): lax.psum_scatter(context, 'member', scatter_dimension=0, tiled=False)  38.7 us
    all_gather x1, waiting for transfers between devices, split_body(): pred_grad = lax.all_gather(own_grad, 'member', axis=0, tiled=True)  30.5 us
    all_gather x1, waiting for transfers between devices, split_body(): student_out = lax.all_gather(student_out_own, 'member', axis=0, tiled=True)  23.7 us
    all_gather x1, waiting for transfers between devices, split_body(): head_all = lax.all_gather(w_head, 'member', axis=1, tiled=True)  20.3 us
    dot_general x1, matrix products, split_body(): jnp.dot(tokens.reshape(images * rows, width), weights, preferred_element_...  16.6 us
  transfers between devices with their start and end apart: 9, of which 8 were waited for; matrix products, arithmetic and copies ran while one was open for 9% of the time, Pallas kernels for 26%

profile of v2, /device:TPU:0, one launch (start us, length us, event | category | flops | bytes accessed | tf_op | source)
XLA Modules:
  0.0 416.6 jit_solution(342212777657419595)
XLA Ops:
  7.2 4.3 %reshape.113 = bf16[344,2,1024]{2,1,0:T(2,128)(2,1)} reshape(bf16[688,1024]{1,0:T(8,128)(2,1)} %param.9) | data formatting | bytes 2818048 | tf_op jit(solution)/shard_map/reshape | solution.py:69
  11.5 1.7 copy.19
  14.2 1.2 pad.8
  15.4 4.3 %reshape.115 = bf16[344,2,1536]{2,1,0:T(2,128)(2,1)S(1)} reshape(bf16[688,1536]{1,0:T(8,128)(2,1)} %param.7) | data formatting | bytes 4227072 | tf_op jit(solution)/shard_map/reshape | solution.py:69
  20.0 1.5 pad.9.src
  22.4 0.7 copy-done.7
  23.2 0.9 fusion.37
  24.3 1.1 copy-done.8
  25.4 2.6 fusion.34
  28.3 108.0 %gather_teacher.1 = (bf16[2,1408,1536]{2,1,0:T(8,128)(2,1)}, bf16[1536,1152]{1,0:T(8,128)(2,1)}) custom-call(bf16[2,352,1536]{2,1,0:T(8,128)(2,1)} %pad.9.src, bf16[1536,1152]{1,0:T(8,128)(2,1)} %bitcast.41), custom_call_target="tpu_custom_call" | custom-call | bytes 276824064 | tf_op jit(solution)/shard_map/gather_teacher/pallas_call | solution.py:188
  136.3 16.6 %convolution_convert_fusion = bf16[2816,1152]{1,0:T(8,128)(2,1)} fusion(bf16[2816,1536]{1,0:T(8,128)(2,1)} %bitcast.44, bf16[1536,1152]{1,0:T(8,128)(2,1)} %get-tuple-element.12), kind=kOutput, calls=%fused_computation | convolution fusion | flops 9968910336 | bytes 18677760 | tf_op jit(solution)/shard_map/dot_general | solution.py:234
  152.9 1.7 add_convert_fusion
  154.8 39.3 %attention.1 = bf16[2,1408,384]{2,1,0:T(8,128)(2,1)S(1)} custom-call(bf16[2,1408,1152]{2,1,0:T(8,128)(2,1)} %bitcast.45, bf16[2,1408,1152]{2,1,0:T(8,128)(2,1)} %bitcast.46, bf16[2,1408,1152]{2,1,0:T(8,128)(2,1)} %bitcast.47, bf16[1408,128]{1,0:T(8,128)(2,1)S(1)} %broadcast_in_dim.35.bias_ref), custom_call_target="tpu_custom_call" | custom-call | flops 12180258816 | bytes 9732096 | tf_op jit(solution)/shard_map/attention/pallas_call | solution.py:51
  194.2 1.6 copy.13
  197.2 38.7 %reduce-scatter.8.cloned.1.call-done = bf16[1,352,384]{2,1,0:T(8,128)(2,1)} async-done(((bf16[8,352,384]{2,1,0:T(8,128)(2,1)}), bf16[1,352,384]{2,1,0:T(8,128)(2,1)}) %reduce-scatter.8.cloned.1.call-update) | async-done | bytes 270352 | tf_op jit(solution)/shard_map/reduce_scatter | solution.py:247
  235.9 4.6 %all-to-all-start = ((bf16[4,88,384]{2,1,0:T(8,128)(2,1)}), bf16[4,88,384]{2,1,0:T(8,128)(2,1)S(1)}, u32[]{:S(2)}, u32[]{:S(2)}) async-start(bf16[4,88,384]{2,1,0:T(8,128)(2,1)} %bitcast.43), calls=%async_computation.2 | async-start | bytes 540672 | tf_op jit(solution)/shard_map/all_to_all | solution.py:248
  240.5 9.1 %all-to-all-done = bf16[4,88,384]{2,1,0:T(8,128)(2,1)S(1)} async-done(((bf16[4,88,384]{2,1,0:T(8,128)(2,1)}), bf16[4,88,384]{2,1,0:T(8,128)(2,1)S(1)}, u32[]{:S(2)}, u32[]{:S(2)}) %all-to-all-start) | async-done | bytes 270368 | tf_op jit(solution)/shard_map/all_to_all | solution.py:248
  249.8 20.3 %all-gather.4.cloned.1.call-done = bf16[1024,1536]{0,1:T(8,128)(2,1)} async-done(((bf16[1024,192]{0,1:T(8,128)(2,1)}), bf16[1024,1536]{0,1:T(8,128)(2,1)}) %all-gather.4.cloned.1.call-update) | async-done | bytes 3145744 | tf_op jit(solution)/shard_map/all_gather | solution.py:231
  270.1 3.7 fusion.4
  273.9 23.7 %all-gather.8.cloned.1.call-done = bf16[704,1024]{1,0:T(8,128)(2,1)} async-done(((bf16[88,1024]{1,0:T(8,128)(2,1)}), bf16[704,1024]{1,0:T(8,128)(2,1)}) %all-gather.8.cloned.1.call-update) | async-done | bytes 1441808 | tf_op jit(solution)/shard_map/all_gather | solution.py:242
  297.6 30.5 %all-gather.6.cloned.1.call-done = bf16[704,1536]{1,0:T(8,128)(2,1)} async-done(((bf16[88,1536]{1,0:T(8,128)(2,1)}), bf16[704,1536]{1,0:T(8,128)(2,1)}) %all-gather.6.cloned.1.call-update) | async-done | bytes 2162704 | tf_op jit(solution)/shard_map/all_gather | solution.py:258
  328.1 3.1 convolution_convert_fusion.4
  331.3 4.4 %convolution_convert_fusion.1 = bf16[704,1024]{1,0:T(8,128)(2,1)S(1)} fusion(bf16[704,1536]{1,0:T(8,128)(2,1)S(1)} %copy-done.6, bf16[1024,1536]{0,1:T(8,128)(2,1)} %all-gather.4.cloned.1.call-done), kind=kOutput, calls=%fused_computation.13 | convolution fusion | flops 2215313408 | bytes 6750208 | tf_op jit(solution)/shard_map/dot_general | solution.py:261
  335.7 1.1 copy-done.10
  336.9 2.1 convolution_convert_fusion.2
  339.1 5.2 %convolution_convert_fusion.3 = bf16[1024,512]{1,0:T(8,128)(2,1)} fusion(bf16[704,1024]{1,0:T(8,128)(2,1)S(1)} %copy-done.4, f32[704,512]{1,0:T(8,128)} %copy-done.8, bf16[704,1024]{1,0:T(8,128)(2,1)} %copy-done.10, bf16[1024,512]{1,0:T(8,128)(2,1)S(1)} %copy-done), kind=kOutput, calls=%fused_computation.15 | convolution fusion | flops 1484128256 | bytes 6422528 | tf_op jit(solution)/shard_map/dot_general | solution.py:270
  344.3 7.7 %reduce-scatter.14.cloned.1.call-done = bf16[256,192]{0,1:T(8,128)(2,1)} async-done(((bf16[1024,192]{0,1:T(8,128)(2,1)}), bf16[256,192]{0,1:T(8,128)(2,1)}) %reduce-scatter.14.cloned.1.call-update) | async-done | bytes 98320 | tf_op jit(solution)/shard_map/reduce_scatter | solution.py:277
  352.0 1.6 convert_element_type.94
  353.6 26.3 %reduce-scatter.12.cloned.1.call-done = bf16[256,512]{1,0:T(8,128)(2,1)} async-done(((bf16[1024,512]{1,0:T(8,128)(2,1)}), bf16[256,512]{1,0:T(8,128)(2,1)}) %reduce-scatter.12.cloned.1.call-update) | async-done | bytes 262160 | tf_op jit(solution)/shard_map/reduce_scatter | solution.py:277
  379.8 1.8 convert_element_type.92
  381.6 26.3 %reduce-scatter.10.cloned.1.call-done = bf16[256,512]{1,0:T(8,128)(2,1)} async-done(((bf16[1024,512]{1,0:T(8,128)(2,1)}), bf16[256,512]{1,0:T(8,128)(2,1)}) %reduce-scatter.10.cloned.1.call-update) | async-done | bytes 262160 | tf_op jit(solution)/shard_map/reduce_scatter | solution.py:277
  408.0 1.8 convert_element_type.90
  (51 shorter events, 4.6 us)
Async XLA Ops:
  7.2 18.2 %copy-start = (bf16[1024,512]{1,0:T(8,128)(2,1)S(1)}, bf16[1024,512]{1,0:T(8,128)(2,1)}, u32[]{:S(2)}) copy-start(bf16[1024,512]{1,0:T(8,128)(2,1)} %param.12) | copy-start | bytes 3145732
  7.2 145.7 %reduce-scatter.6.cloned.1.call-start = ((), (), s32[]{:S(2)}) async-start(), calls=%async_computation.6 | async-start | bytes 3244032 | tf_op jit(solution)/shard_map/reduce_scatter | solution.py:228
  19.9 2.0 copy-start.1
  19.9 2.0 copy-start.5
  21.9 1.2 copy-start.7
  23.2 1.1 copy-start.3
  24.3 1.1 copy-start.8
  28.0 207.8 %reduce-scatter.8.cloned.1.call-start = ((), (), s32[]{:S(2)}) async-start(), calls=%async_computation.8 | async-start | bytes 2433024 | tf_op jit(solution)/shard_map/reduce_scatter | solution.py:247
  195.8 74.3 %all-gather.4.cloned.1.call-start = ((), (), s32[]{:S(2)}) async-start(), calls=%async_computation.7 | async-start | bytes 3538944 | tf_op jit(solution)/shard_map/all_gather | solution.py:231
  196.6 73.5 %copy-start.2 = (bf16[88,1024]{1,0:T(8,128)(2,1)S(1)}, bf16[88,1024]{1,0:T(8,128)(2,1)}, u32[]{:S(2)}) copy-start(bf16[88,1024]{1,0:T(8,128)(2,1)} %add_convert_fusion) | copy-start | bytes 540676
  196.6 101.0 %all-gather.8.cloned.1.call-start = ((), (), s32[]{:S(2)}) async-start(), calls=%async_computation.12 | async-start | bytes 1622016 | tf_op jit(solution)/shard_map/all_gather | solution.py:242
  235.9 13.7 %all-to-all-start = ((bf16[4,88,384]{2,1,0:T(8,128)(2,1)}), bf16[4,88,384]{2,1,0:T(8,128)(2,1)S(1)}, u32[]{:S(2)}, u32[]{:S(2)}) async-start(bf16[4,88,384]{2,1,0:T(8,128)(2,1)} %bitcast.43), calls=%async_computation.2 | async-start | bytes 540672 | tf_op jit(solution)/shard_map/all_to_all | solution.py:248
  240.5 87.7 %all-gather.6.cloned.1.call-start = ((), (), s32[]{:S(2)}) async-start(), calls=%async_computation.9 | async-start | bytes 2433024 | tf_op jit(solution)/shard_map/all_gather | solution.py:258
  273.8 78.2 %reduce-scatter.14.cloned.1.call-start = ((), (), s32[]{:S(2)}) async-start(), calls=%async_computation.13 | async-start | bytes 491520 | tf_op jit(solution)/shard_map/reduce_scatter | solution.py:277
  328.1 3.2 copy-start.6
  331.3 48.6 %reduce-scatter.12.cloned.1.call-start = ((), (), s32[]{:S(2)}) async-start(), calls=%async_computation.11 | async-start | bytes 1310720 | tf_op jit(solution)/shard_map/reduce_scatter | solution.py:277
  331.3 5.5 %copy-start.9 = (f32[704,512]{1,0:T(8,128)S(1)}, f32[704,512]{1,0:T(8,128)}, u32[]{:S(2)}) copy-start(f32[704,512]{1,0:T(8,128)} %copy-done.8) | copy-start | bytes 4325380
  335.7 1.1 copy-start.10
  336.9 2.2 copy-start.4
  339.0 69.0 %reduce-scatter.10.cloned.1.call-start = ((), (), s32[]{:S(2)}) async-start(), calls=%async_computation.10 | async-start | bytes 1310720 | tf_op jit(solution)/shard_map/reduce_scatter | solution.py:277
Sparse Core Ops, SparseCore 0:
  28.1 60.3 reduce-scatter.5
  195.9 39.8 reduce-scatter.7
  237.8 32.2 all-gather.3
  272.4 25.1 all-gather.7
  299.9 28.1 all-gather.5
  331.4 20.5 reduce-scatter.13
  354.4 25.4 reduce-scatter.11
  382.1 25.7 reduce-scatter.9

commit v3 on v2

--- a/solution.py
+++ b/solution.py
@@ -64,24 +64,33 @@
     )(projected, projected, projected, bias)
 
 
-def by_image(tokens, slot_rows):
-    rows, width = tokens.shape
-    split = tokens.reshape(rows // IMAGES, IMAGES, width).transpose(1, 0, 2)
-    return jnp.pad(split, ((0, 0), (0, slot_rows - rows // IMAGES), (0, 0)))
-
-
-def gather_kernel(dp, src, wts, tok, own, z_send, z_recv, p_send, p_recv, f_send, f_recv, w_send, w_recv, local):
-    rows, width = src.shape[1], src.shape[2]
-    depth, piece = wts.shape[0], wts.shape[1] // 3
-    m, z = lax.axis_index("member"), lax.axis_index("dp")
+def by_image(tokens, parts, rows, slots):
+    count = tokens.shape[0]
+    each = parts // IMAGES
+    out = jnp.arange(parts * slots, dtype=jnp.int32)
+    part, at = out // slots, out % slots
+    place = (part % each) * rows + at
+    source = jnp.where((at < rows) & (place < count // IMAGES), place * IMAGES + part // each, -1)
+    pick = (source[:, None] == jnp.arange(count, dtype=jnp.int32)[None, :]).astype(tokens.dtype)
+    return jnp.dot(pick, tokens, preferred_element_type=jnp.float32).astype(tokens.dtype)
+
+
+def plane_peers(m):
     core, x, y = m % 2, (m // 2) % 2, m // 4
-    chips = 4
-    share = width // chips
-    other_core = m + 1 - 2 * core
     to_x, to_y = 2 - 4 * x, 4 - 8 * y
-    peers = [m + to_x, m + to_y, m + to_x + to_y, other_core]
-
+    return [m + to_x, m + to_y, m + to_x + to_y, m + 1 - 2 * core]
+
+
+def remote(source, target, send_sem, recv_sem, member, part):
+    return pltpu.make_async_remote_copy(
+        src_ref=source, dst_ref=target, send_sem=send_sem, recv_sem=recv_sem,
+        device_id={"member": member, "dp": part}, device_id_type=pl.DeviceIdType.MESH,
+    )
+
+
+def greet(m, z, dp):
     barrier = pltpu.get_barrier_semaphore()
+    peers = plane_peers(m)
     for k in range(1, dp):
         pl.semaphore_signal(
             barrier, inc=1, device_id={"member": m, "dp": (z + k) % dp}, device_id_type=pl.DeviceIdType.MESH
@@ -91,6 +100,49 @@
             barrier, inc=1, device_id={"member": peer, "dp": z}, device_id_type=pl.DeviceIdType.MESH
         )
     pl.semaphore_wait(barrier, dp - 1 + len(peers))
+
+
+class PlaneGather:
+    def __init__(self, source, out, m, z, sends, recvs):
+        self.out, self.m, self.z, self.sends, self.recvs = out, m, z, sends, recvs
+        self.peers = plane_peers(m)
+        self.first = [
+            remote(source, out.at[m], sends.at[p], recvs.at[p], self.peers[p], z) for p in range(4)
+        ]
+        self.second = []
+
+    def start(self):
+        for copy in self.first:
+            copy.start()
+
+    def forward(self):
+        for p in range(3):
+            here = self.out.at[self.peers[p]]
+            self.first[p].wait_recv()
+            copy = remote(here, here, self.sends.at[4 + p], self.recvs.at[4 + p], self.peers[3], self.z)
+            copy.start()
+            self.second.append(copy)
+
+    def finish(self):
+        self.first[3].wait_recv()
+        for copy in self.second:
+            copy.wait_recv()
+        for copy in self.first + self.second:
+            copy.wait_send()
+
+
+def gather_kernel(
+    dp, src, wts, head, tok, own, head_all,
+    z_send, z_recv, p_send, p_recv, f_send, f_recv, w_send, w_recv, local, h_send, h_recv,
+):
+    rows, width = src.shape[1], src.shape[2]
+    piece = wts.shape[1] // 3
+    m, z = lax.axis_index("member"), lax.axis_index("dp")
+    core = m % 2
+    share = width // 4
+    peers = plane_peers(m)
+    other_core = peers[3]
+    greet(m, z, dp)
 
     def columns(chip):
         return pl.ds(pl.multiple_of(chip * share, PAIR), share)
@@ -115,23 +167,16 @@
         first.append(copy)
     stay = pltpu.make_async_copy(src, tok.at[:, pl.ds(pl.multiple_of(z * rows, ROWS), rows), :], local.at[3])
     stay.start()
+    head_stay = pltpu.make_async_copy(head, head_all.at[m], local.at[4])
+    head_stay.start()
+    heads = PlaneGather(head, head_all, m, z, h_send, h_recv)
+    heads.start()
 
     def weight_copy(j):
         dest, slot = (3 * z + j) % dp, (3 * z + j) // dp
         source = wts.at[:, pl.ds(j * piece, piece)]
         target = own.at[:, pl.ds(pl.multiple_of(slot * piece, PAIR), piece)]
         return dest, source, target, slot
-
-    for j in range(3):
-        dest, source, target, slot = weight_copy(j)
-
-        @pl.when(dest == z)
-        def _():
-            pltpu.make_async_copy(source, target, local.at[j]).start()
-
-        @pl.when(dest != z)
-        def _():
-            send(source, target, (w_send.at[j], w_recv.at[slot]), m, dest).start()
 
     passed = []
     for k in range(1, dp):
@@ -142,7 +187,21 @@
             copy = send(here, here, (p_send.at[k - 1, p], p_recv.at[k - 1, p]), peer, z)
             copy.start()
             passed.append(copy)
-    chips_of = [(m + to_x) // 2, (m + to_y) // 2, (m + to_x + to_y) // 2]
+    for copy in first:
+        copy.wait_send()
+    for j in range(3):
+        dest, source, target, slot = weight_copy(j)
+
+        @pl.when(dest == z)
+        def _():
+            pltpu.make_async_copy(source, target, local.at[j]).start()
+
+        @pl.when(dest != z)
+        def _():
+            send(source, target, (w_send.at[j], w_recv.at[slot]), m, dest).start()
+
+    heads.forward()
+    chips_of = [peer // 2 for peer in peers[:3]]
     for k in range(1, dp):
         part = (z + dp - k) % dp
         for p in range(3):
@@ -158,7 +217,9 @@
         for p in range(3):
             there = region(1 - core, part, chips_of[p])
             send(there, there, (f_send.at[k - 1, p], f_recv.at[k - 1, p]), other_core, z).wait_recv()
-    for copy in first + passed:
+    heads.finish()
+    head_stay.wait()
+    for copy in passed:
         copy.wait_send()
     for j in range(3):
         dest, source, target, slot = weight_copy(j)
@@ -181,7 +242,7 @@
     stay.wait()
 
 
-def gather_teacher(tokens, weights, dp):
+def gather_teacher(tokens, weights, head, dp, member):
     images, rows, width = tokens.shape
     steps = dp - 1
     dma = pltpu.SemaphoreType.DMA
@@ -190,29 +251,144 @@
         out_shape=(
             jax.ShapeDtypeStruct((images, dp * rows, width), tokens.dtype),
             jax.ShapeDtypeStruct(weights.shape, weights.dtype),
+            jax.ShapeDtypeStruct((member,) + head.shape, head.dtype),
         ),
-        in_specs=[pl.BlockSpec(memory_space=pl.ANY)] * 2,
-        out_specs=(pl.BlockSpec(memory_space=pl.ANY),) * 2,
+        in_specs=[pl.BlockSpec(memory_space=pl.ANY)] * 3,
+        out_specs=(pl.BlockSpec(memory_space=pl.ANY),) * 3,
         scratch_shapes=[
             dma((steps,)), dma((steps,)), dma((steps, 4)), dma((steps, 4)), dma((steps, 3)), dma((steps, 3)),
-            dma((3,)), dma((3,)), dma((4,)),
+            dma((3,)), dma((3,)), dma((5,)), dma((7,)), dma((7,)),
         ],
         compiler_params=pltpu.CompilerParams(collective_id=0, has_side_effects=True),
         cost_estimate=pl.CostEstimate(
             flops=0, bytes_accessed=64 * images * dp * rows * width, transcendentals=0
         ),
         name="gather_teacher",
-    )(tokens, weights)
+    )(tokens, weights, head)
+
+
+def middle_kernel(
+    dp, part_rows, own_rows, norm, context, own_out, head, grads, outs,
+    pair, plane_out, plane_in, z_out, summed, pred, own_grad,
+    c_send, c_recv, p_send, p_recv, z_send, z_recv, g_send, g_recv, o_send, o_recv,
+):
+    m, z = lax.axis_index("member"), lax.axis_index("dp")
+    core, chip = m % 2, m // 2
+    member, share, slots = context.shape[0], context.shape[2], own_out.shape[0]
+    width = head.shape[0]
+    peers = plane_peers(m)
+    f32 = jnp.float32
+    greet(m, z, dp)
+
+    across = [
+        remote(context.at[2 * c + 1 - core], pair.at[c], c_send.at[c], c_recv.at[c], peers[3], z)
+        for c in range(member // 2)
+    ]
+    for copy in across:
+        copy.start()
+    out_gather = PlaneGather(own_out, outs, m, z, o_send, o_recv)
+    for d in range(dp):
+        at = slice(d * share, (d + 1) * share)
+        pred[:, at] = lax.dot_general(
+            own_out[...], head[at, :], (((1,), (1,)), ((), ())), preferred_element_type=f32
+        )
+    outs[pl.ds(m, 1)] = own_out[...][None]
+    for copy in across:
+        copy.wait_recv()
+    in_plane = []
+    for p in range(3):
+        there = peers[p] // 2
+        plane_out[p] = (context[peers[p]].astype(f32) + pair[there].astype(f32)).astype(jnp.bfloat16)
+        copy = remote(plane_out.at[p], plane_in.at[p], p_send.at[p], p_recv.at[p], peers[p], z)
+        copy.start()
+        in_plane.append(copy)
+    out_gather.start()
+    total = context[m].astype(f32) + pair[chip].astype(f32)
+    for p in range(3):
+        in_plane[p].wait_recv()
+        total = total + plane_in[p].astype(f32)
+    fill = jnp.zeros((slots - own_rows, share), f32)
+    for d in range(dp):
+        block = jnp.concatenate([total[d * own_rows : (d + 1) * own_rows], fill], axis=0)
+        z_out[d] = block.astype(jnp.bfloat16)
+    over = []
+    for k in range(1, dp):
+        there = (z + k) % dp
+        copy = remote(z_out.at[there], summed.at[z], z_send.at[k - 1], z_recv.at[k - 1], m, there)
+        copy.start()
+        over.append(copy)
+    summed[pl.ds(z, 1)] = z_out[pl.ds(z, 1)]
+    out_gather.forward()
+    for copy in over:
+        copy.wait_recv()
+    blocks = [summed[d].astype(f32) for d in range(dp)]
+    mean = sum(jnp.sum(b, axis=-1, keepdims=True) for b in blocks) / width
+    square = sum(jnp.sum(b * b, axis=-1, keepdims=True) for b in blocks) / width
+    scale = lax.rsqrt(square - mean * mean + 1e-06)
+    quarter = part_rows_slots(part_rows) // own_rows
+    row = lax.broadcasted_iota(jnp.int32, (slots, share), 0)
+    place = (m % quarter) * own_rows + row
+    real = (row < own_rows) & (place < part_rows) & (z * part_rows + place < VALID)
+    for d in range(dp):
+        at = slice(d * share, (d + 1) * share)
+        target = (blocks[d] - mean) * scale
+        own_grad[:, at] = jnp.where(real, (pred[:, at] - target) / norm, 0.0).astype(jnp.bfloat16)
+    grad_gather = PlaneGather(own_grad, grads, m, z, g_send, g_recv)
+    grad_gather.start()
+    grads[pl.ds(m, 1)] = own_grad[...][None]
+    grad_gather.forward()
+    out_gather.finish()
+    grad_gather.finish()
+    for copy in across + in_plane + over:
+        copy.wait_send()
+
+
+def part_rows_slots(part_rows):
+    return -(-part_rows // ROWS) * ROWS
+
+
+def middle(context, own_out, head, dp, part_rows, own_rows):
+    member, rows, share = context.shape
+    slots, inner = own_out.shape
+    width = head.shape[0]
+    half = member // 2
+    dma = pltpu.SemaphoreType.DMA
+    vmem = lambda *shape: pltpu.VMEM(shape, jnp.bfloat16)
+    whole = pl.BlockSpec(memory_space=pltpu.VMEM)
+    return pl.pallas_call(
+        partial(middle_kernel, dp, part_rows, own_rows, math.sqrt(IMAGES * VALID)),
+        out_shape=(
+            jax.ShapeDtypeStruct((member, slots, width), jnp.bfloat16),
+            jax.ShapeDtypeStruct((member, slots, inner), jnp.bfloat16),
+        ),
+        in_specs=[whole] * 3,
+        out_specs=(whole,) * 2,
+        scratch_shapes=[
+            vmem(half, rows, share), vmem(3, rows, share), vmem(3, rows, share),
+            vmem(dp, slots, share), vmem(dp, slots, share),
+            pltpu.VMEM((slots, width), jnp.float32), vmem(slots, width),
+            dma((half,)), dma((half,)), dma((3,)), dma((3,)), dma((dp - 1,)), dma((dp - 1,)),
+            dma((7,)), dma((7,)), dma((7,)), dma((7,)),
+        ],
+        compiler_params=pltpu.CompilerParams(
+            collective_id=1, has_side_effects=True, vmem_limit_bytes=48 * 1024 * 1024
+        ),
+        cost_estimate=pl.CostEstimate(
+            flops=2 * slots * width * inner, bytes_accessed=100 * 1024 * 1024, transcendentals=0
+        ),
+        name="context_to_pred_grad",
+    )(context, own_out, head)
 
 
 def split_body(dp, member, teacher_tokens, teacher_qkv, student_tokens, student_gain, w_up, w_down, w_head):
     part_rows = teacher_tokens.shape[0] // IMAGES
-    slot_rows = -(-part_rows // ROWS) * ROWS
+    slot_rows = part_rows_slots(part_rows)
     own_rows = IMAGES * slot_rows // member
+    own_slots = part_rows_slots(own_rows)
     quarter = slot_rows // own_rows
-    dp_at, member_at = lax.axis_index("dp"), lax.axis_index("member")
-
-    student = by_image(student_tokens, slot_rows).reshape(IMAGES * slot_rows, -1)
+    member_at = lax.axis_index("member")
+
+    student = by_image(student_tokens, member, own_rows, own_slots)
     inputs = student.astype(jnp.float32)
     in_mean = jnp.mean(inputs, axis=-1, keepdims=True)
     in_var = jnp.mean((inputs - in_mean) ** 2, axis=-1, keepdims=True)
@@ -223,12 +399,13 @@
     branch_part = lax.dot_general(
         hidden, w_down, (((1,), (1,)), ((), ())), preferred_element_type=jnp.float32
     )
-    teacher_slots, branch_part = lax.optimization_barrier((by_image(teacher_tokens, slot_rows), branch_part))
-    tokens, weights = gather_teacher(teacher_slots, teacher_qkv[0], dp)
+    teacher_slots, branch_part = lax.optimization_barrier((by_image(teacher_tokens, IMAGES, slot_rows, slot_rows), branch_part))
+    teacher_slots = teacher_slots.reshape(IMAGES, slot_rows, -1)
+    tokens, weights, head_all = gather_teacher(teacher_slots, teacher_qkv[0], w_head.T, dp, member)
+    head_all = head_all.reshape(-1, w_head.shape[0])
     branch = lax.psum_scatter(branch_part, "member", scatter_dimension=0, tiled=True)
-    own_inputs = lax.dynamic_slice_in_dim(student, member_at * own_rows, own_rows, 0).astype(jnp.float32)
+    own_inputs = lax.dynamic_slice_in_dim(student, member_at * own_slots, own_slots, 0).astype(jnp.float32)
     own_out = (own_inputs + branch).astype(jnp.bfloat16)
-    head_all = lax.all_gather(w_head, "member", axis=1, tiled=True)
 
     images, rows, width = tokens.shape
     projected = jnp.dot(
@@ -238,28 +415,18 @@
     in_part = key_row % slot_rows
     real_key = (in_part < part_rows) & (key_row // slot_rows * part_rows + in_part < VALID)
     bias = jnp.broadcast_to(jnp.where(real_key, 0.0, -1e30).astype(jnp.bfloat16)[:, None], (rows, PAIR))
-    projected, student_out_own = lax.optimization_barrier((projected, own_out))
-    student_out = lax.all_gather(student_out_own, "member", axis=0, tiled=True)
     context = attention(projected, bias)
     share = context.shape[-1]
     context = context.reshape(images, dp, quarter, own_rows, share).transpose(0, 2, 1, 3, 4)
     context = context.reshape(member, dp * own_rows, share)
-    summed = lax.psum_scatter(context, "member", scatter_dimension=0, tiled=False)
-    summed = lax.all_to_all(summed.reshape(dp, own_rows, share), "dp", 0, 0, tiled=False)
-    summed = summed.transpose(1, 0, 2).reshape(own_rows, width).astype(jnp.float32)
-    row_mean = jnp.mean(summed, axis=-1, keepdims=True)
-    mean_square = jnp.mean(summed * summed, axis=-1, keepdims=True)
-    target = (summed - row_mean) * lax.rsqrt(mean_square - row_mean * row_mean + 1e-06)
-
-    own_row = (member_at % quarter) * own_rows + jnp.arange(own_rows, dtype=jnp.int32)
-    real = (own_row < part_rows) & (dp_at * part_rows + own_row < VALID)
-    pred = jnp.dot(own_out, head_all, preferred_element_type=jnp.float32)
-    own_grad = jnp.where(real[:, None], (pred - target) / math.sqrt(IMAGES * VALID), 0.0).astype(jnp.bfloat16)
-    pred_grad = lax.all_gather(own_grad, "member", axis=0, tiled=True)
+    pred_grad, student_out = middle(context, own_out, head_all, dp, part_rows, own_rows)
+    pred_grad = pred_grad.reshape(member * own_slots, width)
+    student_out = student_out.reshape(member * own_slots, -1)
+
     head_width = w_head.shape[1]
     own_columns = lax.dynamic_slice_in_dim(pred_grad, member_at * head_width, head_width, 1)
     out_grad = lax.dot_general(
-        pred_grad, head_all, (((1,), (1,)), ((), ())), preferred_element_type=jnp.float32
+        pred_grad, head_all, (((1,), (0,)), ((), ())), preferred_element_type=jnp.float32
     ).astype(jnp.bfloat16)
     grad_down = lax.dot_general(
         out_grad, hidden, (((0,), (0,)), ((), ())), preferred_element_type=jnp.float32

time: 417 us -> 334 us (0.80)
  waiting for transfers between devices: 184 us -> 55.9 us
  Pallas kernels: 147 us -> 207 us
  local copies, waits for them, and re-layouts: 19 us -> 4.72 us
  matrix products: 38.6 us -> 45.5 us
  starting transfers between devices: 5.29 us -> 0.34 us
    all_gather x3 -> x0, waiting for transfers between devices: 74.5 us -> none  [the longest x1 30.5 us: split_body(): pred_grad = lax.all_gather(own_grad, 'member', axis=0, tiled=True)]
    pallas_call x0 -> x1, Pallas kernels: none -> 47.1 us  [middle(): pl.pallas_call(partial(middle_kernel, dp, part_rows, own_rows, math.sqrt(...]
    reduce_scatter x1 -> x0, waiting for transfers between devices: 38.7 us -> none  [split_body(): lax.psum_scatter(context, 'member', scatter_dimension=0, tiled=False)]
    pallas_call x1, Pallas kernels: 108 us -> 120 us  [gather_teacher(): pl.pallas_call(partial(gather_kernel, dp), out_shape=(jax.ShapeDtypeStruc...]
    reshape x4 -> x0, local copies, waits for them, and re-layouts: 10.5 us -> none  [by_image(): split = tokens.reshape(rows // IMAGES, IMAGES, width).transpose(1, 0, 2)]
    all_to_all x1 -> x0, waiting for transfers between devices: 9.07 us -> none  [split_body(): lax.all_to_all(summed.reshape(dp, own_rows, share), 'dp', 0, 0, tiled=False)]
    all_to_all x1 -> x0, starting transfers between devices: 4.6 us -> none  [split_body(): lax.all_to_all(summed.reshape(dp, own_rows, share), 'dp', 0, 0, tiled=False)]
    dot_general x2 -> x3, matrix products: 8.1 us -> 12.7 us  [the longest x1 6.38 us: split_body(): lax.dot_general(pred_grad, head_all, (((1,), (0,)), ((), ())), preferred_...]
  transfers between devices with their start and end apart: 9 -> 4, of which waited for: 8 -> 3; matrix products, arithmetic and copies ran while one was open for 9% -> 11% of each run, Pallas kernels for 26% -> 48%
where the time goes in v3:
time: 334 us
  Pallas kernels  207 us (62%)
  waiting for transfers between devices  55.9 us (17%)
  matrix products  45.5 us (14%)
  between operations  13.9 us (4%)
  other arithmetic  6.89 us (2%)
  local copies, waits for them, and re-layouts  4.72 us (1%)
    pallas_call x1, Pallas kernels, gather_teacher(): pl.pallas_call(partial(gather_kernel, dp), out_shape=(jax.ShapeDtypeStruc...  120 us
    reduce_scatter x3, waiting for transfers between devices, split_body(): lax.psum_scatter(g.astype(jnp.bfloat16), 'dp', scatter_dimension=0, tiled...  55.8 us
    pallas_call x1, Pallas kernels, middle(): pl.pallas_call(partial(middle_kernel, dp, part_rows, own_rows, math.sqrt(...  47.1 us
    pallas_call x1, Pallas kernels, attention(): pl.pallas_call(partial(attention_kernel, tile), grid=(images, pairs), in_...  39.6 us
    dot_general x1, matrix products, split_body(): jnp.dot(tokens.reshape(images * rows, width), weights, preferred_element_...  16.6 us
  transfers between devices with their start and end apart: 4, of which 3 were waited for; matrix products, arithmetic and copies ran while one was open for 11% of the time, Pallas kernels for 48%

profile of v3, /device:TPU:0, one launch (start us, length us, event | category | flops | bytes accessed | tf_op | source)
XLA Modules:
  0.0 333.9 jit_solution(10429794244873773490)
XLA Ops:
  7.2 0.0 reduce-scatter.5.cloned.1.call-start
  7.3 3.0 convert_reduce_fusion
  10.3 0.6 fusion.2
  10.9 3.3 convolution_convert_fusion.1
  14.2 1.0 fusion.67
  15.3 1.2 copy-done.6
  16.5 2.7 fusion.65
  19.2 0.0 reduce-scatter.5.cloned.1.call-update
  19.2 0.2 reduce-scatter.11.cloned.1.call-start
  19.5 120.0 %gather_teacher.1 = (bf16[2,1408,1536]{2,1,0:T(8,128)(2,1)}, bf16[1536,1152]{1,0:T(8,128)(2,1)}, bf16[8,192,1024]{2,1,0:T(8,128)(2,1)}) custom-call(bf16[2,352,1536]{2,1,0:T(8,128)(2,1)} %bitcast.30, bf16[1536,1152]{1,0:T(8,128)(2,1)} %bitcast.27, bf16[192,1024]{1,0:T(8,128)(2,1)} %bitcast.31), custom_call_target="tpu_custom_call" | custom-call | bytes 276824064 | tf_op jit(solution)/shard_map/gather_teacher/pallas_call | solution.py:249
  139.5 16.6 %convolution_convert_fusion = bf16[2816,1152]{1,0:T(8,128)(2,1)} fusion(bf16[2816,1536]{1,0:T(8,128)(2,1)} %bitcast.32, bf16[1536,1152]{1,0:T(8,128)(2,1)} %get-tuple-element.12), kind=kOutput, calls=%fused_computation | convolution fusion | flops 9968910336 | bytes 18677760 | tf_op jit(solution)/shard_map/dot_general | solution.py:411
  156.1 0.2 broadcast_in_dim.16.bias_ref
  156.4 39.6 %attention.1 = bf16[2,1408,384]{2,1,0:T(8,128)(2,1)S(1)} custom-call(bf16[2,1408,1152]{2,1,0:T(8,128)(2,1)} %bitcast.35, bf16[2,1408,1152]{2,1,0:T(8,128)(2,1)} %bitcast.36, bf16[2,1408,1152]{2,1,0:T(8,128)(2,1)} %bitcast.37, bf16[1408,128]{1,0:T(8,128)(2,1)S(1)} %broadcast_in_dim.16.bias_ref), custom_call_target="tpu_custom_call" | custom-call | flops 12180258816 | bytes 9732096 | tf_op jit(solution)/shard_map/attention/pallas_call | solution.py:51
  196.0 1.6 copy.10
  197.6 1.1 add_convert_fusion.own_out
  198.7 1.6 copy-done.1
  200.3 47.1 %context_to_pred_grad.1 = (bf16[8,96,1536]{2,1,0:T(8,128)(2,1)}, bf16[8,96,1024]{2,1,0:T(8,128)(2,1)S(1)}) custom-call(bf16[8,352,384]{2,1,0:T(8,128)(2,1)S(1)} %bitcast.24, bf16[96,1024]{1,0:T(8,128)(2,1)S(1)} %add_convert_fusion.own_out, bf16[1536,1024]{1,0:T(8,128)(2,1)} %bitcast.28), custom_call_target="tpu_custom_call" | custom-call | flops 301989888 | bytes 104857600 | tf_op jit(solution)/shard_map/context_to_pred_grad/pallas_call | solution.py:358
  247.4 2.5 convolution_convert_fusion.5
  250.0 0.0 reduce-scatter.11.cloned.1.call-update
  250.0 0.0 reduce-scatter.7.cloned.1.call-start
  250.0 6.4 %convolution_convert_fusion.2 = bf16[768,1024]{1,0:T(8,128)(2,1)} fusion(bf16[768,1536]{1,0:T(8,128)(2,1)} %bitcast.34, bf16[1536,1024]{1,0:T(8,128)(2,1)} %bitcast.29), kind=kOutput, calls=%fused_computation.15 | convolution fusion | flops 2416705536 | bytes 7077888 | tf_op jit(solution)/shard_map/dot_general | solution.py:428
  256.4 5.9 %convolution_convert_fusion.4 = bf16[1024,512]{1,0:T(8,128)(2,1)} fusion(f32[768,512]{1,0:T(8,128)} %copy-done.6, bf16[768,1024]{1,0:T(8,128)(2,1)} %copy-done.2, f32[1024]{0:T(1024)S(1)} %copy-done.5, f32[768]{0:T(1024)S(1)} %add_rsqrt_fusion, f32[768]{0:T(1024)S(1)} %broadcast_multiply_fusion, bf16[768,1024]{1,0:T(8,128)(2,1)} %convolution_convert_fusion.2, ...), kind=kOutput, calls=%fused_computation.25 | convolution fusion | flops 1622933504 | bytes 6825984 | tf_op jit(solution)/shard_map/dot_general | solution.py:437
  262.3 0.0 reduce-scatter.7.cloned.1.call-update
  262.3 0.0 reduce-scatter.9.cloned.1.call-start
  262.3 4.0 %convolution_convert_fusion.3 = bf16[1024,512]{1,0:T(8,128)(2,1)} fusion(bf16[768,1024]{1,0:T(8,128)(2,1)} %convolution_convert_fusion.2, f32[768,512]{1,0:T(8,128)} %copy-done.6), kind=kOutput, calls=%fused_computation.24 | convolution fusion | flops 809369600 | bytes 4194304 | tf_op jit(solution)/shard_map/dot_general | solution.py:431
  266.4 0.0 reduce-scatter.9.cloned.1.call-update
  266.4 3.4 %reduce-scatter.11.cloned.1.call-done = bf16[256,192]{0,1:T(8,128)(2,1)} async-done(((bf16[1024,192]{0,1:T(8,128)(2,1)}), bf16[256,192]{0,1:T(8,128)(2,1)}) %reduce-scatter.11.cloned.1.call-update) | async-done | bytes 98320 | tf_op jit(solution)/shard_map/reduce_scatter | solution.py:444
  269.7 1.6 convert_element_type.73
  271.3 26.2 %reduce-scatter.7.cloned.1.call-done = bf16[256,512]{1,0:T(8,128)(2,1)} async-done(((bf16[1024,512]{1,0:T(8,128)(2,1)}), bf16[256,512]{1,0:T(8,128)(2,1)}) %reduce-scatter.7.cloned.1.call-update) | async-done | bytes 262160 | tf_op jit(solution)/shard_map/reduce_scatter | solution.py:444
  297.5 1.8 convert_element_type.69
  299.3 26.3 %reduce-scatter.9.cloned.1.call-done = bf16[256,512]{1,0:T(8,128)(2,1)} async-done(((bf16[1024,512]{1,0:T(8,128)(2,1)}), bf16[256,512]{1,0:T(8,128)(2,1)}) %reduce-scatter.9.cloned.1.call-update) | async-done | bytes 262160 | tf_op jit(solution)/shard_map/reduce_scatter | solution.py:444
  325.6 1.8 convert_element_type.71
  (18 shorter events, 0.1 us)
Async XLA Ops:
  7.2 3.7 %copy-start = (bf16[688,1536]{1,0:T(8,128)(2,1)S(1)}, bf16[688,1536]{1,0:T(8,128)(2,1)}, u32[]{:S(2)}) copy-start(bf16[688,1536]{1,0:T(8,128)(2,1)} %param.7) | copy-start | bytes 6340612
  7.2 190.4 %reduce-scatter.5.cloned.1.call-start = ((), (), s32[]{:S(2)}) async-start(), calls=%async_computation.4 | async-start | bytes 3538944 | tf_op jit(solution)/shard_map/reduce_scatter | solution.py:406
  10.3 3.9 %copy-start.2 = (bf16[768,1024]{1,0:T(8,128)(2,1)}, bf16[768,1024]{1,0:T(8,128)(2,1)S(1)}, u32[]{:S(2)}) copy-start(bf16[768,1024]{1,0:T(8,128)(2,1)S(1)} %get-tuple-element.18) | copy-start | bytes 4718596
  10.9 3.3 copy-start.3
  10.9 3.3 copy-start.5
  14.2 2.3 copy-start.4
  15.3 1.2 copy-start.6
  19.2 250.5 %reduce-scatter.11.cloned.1.call-start = ((), (), s32[]{:S(2)}) async-start(), calls=%async_computation.7 | async-start | bytes 491520 | tf_op jit(solution)/shard_map/reduce_scatter | solution.py:444
  198.7 1.6 copy-start.1
  250.0 47.5 %reduce-scatter.7.cloned.1.call-start = ((), (), s32[]{:S(2)}) async-start(), calls=%async_computation.5 | async-start | bytes 1310720 | tf_op jit(solution)/shard_map/reduce_scatter | solution.py:444
  262.3 63.3 %reduce-scatter.9.cloned.1.call-start = ((), (), s32[]{:S(2)}) async-start(), calls=%async_computation.6 | async-start | bytes 1310720 | tf_op jit(solution)/shard_map/reduce_scatter | solution.py:444
Sparse Core Ops, SparseCore 0:
  19.4 70.6 reduce-scatter.4
  250.1 19.5 reduce-scatter.10
  272.0 25.3 reduce-scatter.6
  299.7 25.7 reduce-scatter.8

commit v4 on v3

--- a/solution.py
+++ b/solution.py
@@ -403,6 +403,7 @@
     teacher_slots = teacher_slots.reshape(IMAGES, slot_rows, -1)
     tokens, weights, head_all = gather_teacher(teacher_slots, teacher_qkv[0], w_head.T, dp, member)
     head_all = head_all.reshape(-1, w_head.shape[0])
+    tokens, branch_part = lax.optimization_barrier((tokens, branch_part))
     branch = lax.psum_scatter(branch_part, "member", scatter_dimension=0, tiled=True)
     own_inputs = lax.dynamic_slice_in_dim(student, member_at * own_slots, own_slots, 0).astype(jnp.float32)
     own_out = (own_inputs + branch).astype(jnp.bfloat16)
@@ -423,27 +424,30 @@
     pred_grad = pred_grad.reshape(member * own_slots, width)
     student_out = student_out.reshape(member * own_slots, -1)
 
+    def scatter(grad):
+        return lax.psum_scatter(grad, "dp", scatter_dimension=0, tiled=True).astype(jnp.float32)
+
+    def tokens_product(left, right):
+        product = lax.dot_general(left, right, (((0,), (0,)), ((), ())), preferred_element_type=jnp.float32)
+        return product.astype(jnp.bfloat16)
+
     head_width = w_head.shape[1]
     own_columns = lax.dynamic_slice_in_dim(pred_grad, member_at * head_width, head_width, 1)
+    grad_head = tokens_product(student_out, own_columns)
+    pred_grad, grad_head = lax.optimization_barrier((pred_grad, grad_head))
+    grad_head = scatter(grad_head)
     out_grad = lax.dot_general(
         pred_grad, head_all, (((1,), (0,)), ((), ())), preferred_element_type=jnp.float32
     ).astype(jnp.bfloat16)
-    grad_down = lax.dot_general(
-        out_grad, hidden, (((0,), (0,)), ((), ())), preferred_element_type=jnp.float32
-    )
+    grad_down = tokens_product(out_grad, hidden)
+    out_grad, grad_down = lax.optimization_barrier((out_grad, grad_down))
+    out_grad, grad_head = lax.optimization_barrier((out_grad, grad_head))
+    grad_down = scatter(grad_down)
     hidden_grad = jnp.dot(out_grad, w_down, preferred_element_type=jnp.float32)
     _, pullback = jax.vjp(gelu_tanh, pre)
     pre_grad = pullback(hidden_grad)[0].astype(jnp.bfloat16)
-    grad_up = lax.dot_general(
-        normed, pre_grad, (((0,), (0,)), ((), ())), preferred_element_type=jnp.float32
-    )
-    grad_head = lax.dot_general(
-        student_out, own_columns, (((0,), (0,)), ((), ())), preferred_element_type=jnp.float32
-    )
-    return tuple(
-        lax.psum_scatter(g.astype(jnp.bfloat16), "dp", scatter_dimension=0, tiled=True).astype(jnp.float32)
-        for g in (grad_up, grad_down, grad_head)
-    )
+    grad_up = scatter(tokens_product(normed, pre_grad))
+    return grad_up, grad_down, grad_head
 
 
 def body(teacher_tokens, teacher_qkv, student_tokens, student_gain, w_up, w_down, w_head):

time: 334 us -> 335 us (level)
  transfers between devices with their start and end apart: 4 -> 4, of which waited for: 3 -> 3; matrix products, arithmetic and copies ran while one was open for 11% -> 11% of each run, Pallas kernels for 48% -> 12%
where the time goes in v4:
time: 335 us
  Pallas kernels  207 us (62%)
  waiting for transfers between devices  57.6 us (17%)
  matrix products  42.6 us (13%)
  between operations  13.9 us (4%)
  local copies, waits for them, and re-layouts  7.07 us (2%)
  other arithmetic  6.89 us (2%)
    pallas_call x1, Pallas kernels, gather_teacher(): pl.pallas_call(partial(gather_kernel, dp), out_shape=(jax.ShapeDtypeStruc...  120 us
    reduce_scatter x3, waiting for transfers between devices, scatter(): lax.psum_scatter(grad, 'dp', scatter_dimension=0, tiled=True)  57.5 us
    pallas_call x1, Pallas kernels, middle(): pl.pallas_call(partial(middle_kernel, dp, part_rows, own_rows, math.sqrt(...  47.1 us
    pallas_call x1, Pallas kernels, attention(): pl.pallas_call(partial(attention_kernel, tile), grid=(images, pairs), in_...  39.6 us
    dot_general x1, matrix products, split_body(): jnp.dot(tokens.reshape(images * rows, width), weights, preferred_element_...  16.6 us
    dot_general x3, matrix products, tokens_product(): lax.dot_general(left, right, (((0,), (0,)), ((), ())), preferred_element_...  10.6 us
  transfers between devices with their start and end apart: 4, of which 3 were waited for; matrix products, arithmetic and copies ran while one was open for 11% of the time, Pallas kernels for 12%

profile of v4, /device:TPU:0, one launch (start us, length us, event | category | flops | bytes accessed | tf_op | source)
XLA Modules:
  0.0 335.0 jit_solution(13678281317990732130)
XLA Ops:
  7.2 0.0 reduce-scatter.5.cloned.1.call-start
  7.3 3.0 convert_reduce_fusion
  10.3 0.6 fusion.2
  10.9 1.2 copy-done.3
  12.1 1.0 fusion.67
  13.1 1.3 copy-done.6
  14.4 2.7 fusion.65
  17.1 3.3 convolution_convert_fusion.1
  20.4 120.0 %gather_teacher.1 = (bf16[2,1408,1536]{2,1,0:T(8,128)(2,1)}, bf16[1536,1152]{1,0:T(8,128)(2,1)}, bf16[8,192,1024]{2,1,0:T(8,128)(2,1)}) custom-call(bf16[2,352,1536]{2,1,0:T(8,128)(2,1)} %bitcast.30, bf16[1536,1152]{1,0:T(8,128)(2,1)} %bitcast.27, bf16[192,1024]{1,0:T(8,128)(2,1)} %bitcast.31), custom_call_target="tpu_custom_call" | custom-call | bytes 276824064 | tf_op jit(solution)/shard_map/gather_teacher/pallas_call | solution.py:249
  140.4 0.0 reduce-scatter.5.cloned.1.call-update
  140.4 0.2 reduce-scatter.7.cloned.1.call-start
  140.7 16.6 %convolution_convert_fusion = bf16[2816,1152]{1,0:T(8,128)(2,1)} fusion(bf16[2816,1536]{1,0:T(8,128)(2,1)} %bitcast.32, bf16[1536,1152]{1,0:T(8,128)(2,1)} %get-tuple-element.22), kind=kOutput, calls=%fused_computation | convolution fusion | flops 9968910336 | bytes 18677760 | tf_op jit(solution)/shard_map/dot_general | solution.py:412
  157.3 0.2 broadcast_in_dim.16.bias_ref
  157.6 39.6 %attention.1 = bf16[2,1408,384]{2,1,0:T(8,128)(2,1)S(1)} custom-call(bf16[2,1408,1152]{2,1,0:T(8,128)(2,1)} %bitcast.35, bf16[2,1408,1152]{2,1,0:T(8,128)(2,1)} %bitcast.36, bf16[2,1408,1152]{2,1,0:T(8,128)(2,1)} %bitcast.37, bf16[1408,128]{1,0:T(8,128)(2,1)S(1)} %broadcast_in_dim.16.bias_ref), custom_call_target="tpu_custom_call" | custom-call | flops 12180258816 | bytes 9732096 | tf_op jit(solution)/shard_map/attention/pallas_call | solution.py:51
  197.2 1.6 copy.10
  198.8 1.1 add_convert_fusion.own_out
  199.9 1.6 copy-done.1
  201.5 47.1 %context_to_pred_grad.1 = (bf16[8,96,1536]{2,1,0:T(8,128)(2,1)}, bf16[8,96,1024]{2,1,0:T(8,128)(2,1)S(1)}) custom-call(bf16[8,352,384]{2,1,0:T(8,128)(2,1)S(1)} %bitcast.24, bf16[96,1024]{1,0:T(8,128)(2,1)S(1)} %add_convert_fusion.own_out, bf16[1536,1024]{1,0:T(8,128)(2,1)} %bitcast.28), custom_call_target="tpu_custom_call" | custom-call | flops 301989888 | bytes 104857600 | tf_op jit(solution)/shard_map/context_to_pred_grad/pallas_call | solution.py:358
  248.5 2.5 convolution_convert_fusion.5
  251.1 0.0 reduce-scatter.7.cloned.1.call-update
  251.1 0.0 reduce-scatter.11.cloned.1.call-start
  251.2 5.3 %convolution_convert_fusion.2 = bf16[768,1024]{1,0:T(8,128)(2,1)S(1)} fusion(bf16[768,1536]{1,0:T(8,128)(2,1)} %bitcast.34, bf16[1536,1024]{1,0:T(8,128)(2,1)} %bitcast.29), kind=kOutput, calls=%fused_computation.15 | convolution fusion | flops 2416705536 | bytes 7077888 | tf_op jit(solution)/shard_map/dot_general | solution.py:439
  256.5 1.1 copy-done.8
  257.6 2.1 convolution_convert_fusion.4
  259.8 0.0 reduce-scatter.9.cloned.1.call-start
  259.8 11.0 %reduce-scatter.7.cloned.1.call-done = bf16[256,192]{0,1:T(8,128)(2,1)} async-done(((bf16[1024,192]{0,1:T(8,128)(2,1)}), bf16[256,192]{0,1:T(8,128)(2,1)}) %reduce-scatter.7.cloned.1.call-update) | async-done | bytes 98320 | tf_op jit(solution)/shard_map/reduce_scatter | solution.py:428
  270.9 1.6 convert_element_type.69
  272.4 5.9 %convolution_convert_fusion.3 = bf16[1024,512]{1,0:T(8,128)(2,1)} fusion(f32[768,512]{1,0:T(8,128)} %copy-done.6, bf16[768,1024]{1,0:T(8,128)(2,1)} %copy-done.2, f32[1024]{0:T(1024)S(1)} %copy-done.5, f32[768]{0:T(1024)S(1)} %add_rsqrt_fusion, f32[768]{0:T(1024)S(1)} %broadcast_multiply_fusion, bf16[768,1024]{1,0:T(8,128)(2,1)} %copy-done.8, ...), kind=kOutput, calls=%fused_computation.24 | convolution fusion | flops 1622933504 | bytes 6825984 | tf_op jit(solution)/shard_map/dot_general | solution.py:431
  278.4 20.2 %reduce-scatter.11.cloned.1.call-done = bf16[256,512]{1,0:T(8,128)(2,1)} async-done(((bf16[1024,512]{1,0:T(8,128)(2,1)}), bf16[256,512]{1,0:T(8,128)(2,1)}) %reduce-scatter.11.cloned.1.call-update) | async-done | bytes 262160 | tf_op jit(solution)/shard_map/reduce_scatter | solution.py:428
  298.6 1.8 convert_element_type.73
  300.4 26.3 %reduce-scatter.9.cloned.1.call-done = bf16[256,512]{1,0:T(8,128)(2,1)} async-done(((bf16[1024,512]{1,0:T(8,128)(2,1)}), bf16[256,512]{1,0:T(8,128)(2,1)}) %reduce-scatter.9.cloned.1.call-update) | async-done | bytes 262160 | tf_op jit(solution)/shard_map/reduce_scatter | solution.py:428
  326.7 1.8 convert_element_type.72
  (22 shorter events, 0.1 us)
Async XLA Ops:
  7.2 10.0 %copy-start = (bf16[688,1536]{1,0:T(8,128)(2,1)S(1)}, bf16[688,1536]{1,0:T(8,128)(2,1)}, u32[]{:S(2)}) copy-start(bf16[688,1536]{1,0:T(8,128)(2,1)} %param.7) | copy-start | bytes 6340612
  7.2 191.6 %reduce-scatter.5.cloned.1.call-start = ((), (), s32[]{:S(2)}) async-start(), calls=%async_computation.4 | async-start | bytes 3538944 | tf_op jit(solution)/shard_map/reduce_scatter | solution.py:407
  10.3 2.9 copy-start.2
  10.3 1.8 copy-start.3
  10.3 1.8 copy-start.5
  12.1 2.3 copy-start.4
  13.1 1.3 copy-start.6
  140.4 130.4 %reduce-scatter.7.cloned.1.call-start = ((), (), s32[]{:S(2)}) async-start(), calls=%async_computation.5 | async-start | bytes 491520 | tf_op jit(solution)/shard_map/reduce_scatter | solution.py:428
  199.8 1.6 copy-start.1
  251.1 47.5 %reduce-scatter.11.cloned.1.call-start = ((), (), s32[]{:S(2)}) async-start(), calls=%async_computation.7 | async-start | bytes 1310720 | tf_op jit(solution)/shard_map/reduce_scatter | solution.py:428
  251.2 6.5 %copy-start.7 = (f32[768,512]{1,0:T(8,128)S(1)}, f32[768,512]{1,0:T(8,128)}, u32[]{:S(2)}) copy-start(f32[768,512]{1,0:T(8,128)} %copy-done.6) | copy-start | bytes 4718596
  256.5 1.2 copy-start.8
  259.8 66.9 %reduce-scatter.9.cloned.1.call-start = ((), (), s32[]{:S(2)}) async-start(), calls=%async_computation.6 | async-start | bytes 1310720 | tf_op jit(solution)/shard_map/reduce_scatter | solution.py:428
Sparse Core Ops, SparseCore 0:
  140.6 44.4 reduce-scatter.4
  251.2 19.5 reduce-scatter.6
  273.2 25.3 reduce-scatter.10
  300.9 25.8 reduce-scatter.8
